TPU v7x, 128 devices: a whole 4x4x4 slice. The times are simulated.
128 devices in a mesh: dp: 32 (over y, x_lo, z), row: 4 (over x_hi, core).
Axes of the slice: x: 4 (x_hi: 2, x_lo: 2; x = x_hi * 2 + x_lo), y: 4, z: 4, core: 2. Of those that a mesh axis runs over, the one named last changes fastest.
Arguments:
- text: bfloat16 [65536, 1152], P('dp')
- image: bfloat16 [65536, 1152], P(('dp', 'row'))
- positive: int32 [32, 2048], P('dp'), may hold values from 0 to 2047, as said below
- log_temp: float32 [1], replicated, may hold values from 1.8 to 2.8
- bias: float32 [1], replicated, may hold values from -8 to -5
Outputs:
- grad_text: float32 [65536, 1152], P(('dp', 'row'))
- grad_image: float32 [65536, 1152], P(('dp', 'row'))
- loss: float32 [1], replicated
- grad_log_temp: float32 [1], replicated
- grad_bias: float32 [1], replicated
Inputs may be any that keep to these rules, and one draw needn't show every extreme that they name: Each row positive[b] names every image row 0 .. 2047 of block b exactly once.
All inputs are finite; a program needn't handle non-finite values.
Results may differ from a plain program's by a relative error of at most 0.003.
Values may be sent and summed in bfloat16 or wider, within the bound.
A program may use at most 128 MiB of HBM per device.

v0:
```python
import jax
import jax.numpy as jnp
from jax import lax
from jax.sharding import PartitionSpec as P


def shifted(x, axis, by):
    count = lax.axis_size(axis)
    return lax.ppermute(x, axis, [(i, (i + by) % count) for i in range(count)])


def unit_rows(values):
    full = values.astype(jnp.float32)
    inverse = lax.rsqrt(jnp.sum(full * full, axis=-1, keepdims=True) + 1e-06)
    return (full * inverse, inverse)


def unit_backward(grad_unit, unit, inverse):
    along = jnp.sum(unit * grad_unit, axis=-1, keepdims=True)
    return (grad_unit - unit * along) * inverse


def meeting(text_low, image_low, label, temp, shift):
    cosine = lax.dot_general(
        text_low, image_low, (((1,), (1,)), ((), ())), preferred_element_type=jnp.float32
    )
    logits = temp * cosine + shift
    pair_loss = jax.nn.softplus(jnp.where(label > 0.5, -logits, logits))
    slope = jax.nn.sigmoid(logits) - label
    sums = jnp.stack([jnp.sum(pair_loss), jnp.sum(slope * cosine), jnp.sum(slope)])
    slope_low = slope.astype(jnp.bfloat16)
    text_term = temp * jnp.dot(slope_low, image_low, preferred_element_type=jnp.float32)
    image_term = temp * lax.dot_general(
        slope_low, text_low, (((0,), (0,)), ((), ())), preferred_element_type=jnp.float32
    )
    return (text_term, image_term, sums)


def on_device(text, image, positive, log_temp, bias):
    temp = jnp.exp(log_temp[0])
    shift = bias[0]
    rows = image.shape[0]
    block_rows = text.shape[0]
    row_index = lax.axis_index("row")
    first_row = row_index * rows
    text_unit, text_inv = unit_rows(text)
    text_low = text_unit.astype(jnp.bfloat16)
    own_unit = lax.dynamic_slice_in_dim(text_unit, first_row, rows, 0)
    own_inv = lax.dynamic_slice_in_dim(text_inv, first_row, rows, 0)
    image_unit, image_inv = unit_rows(image)
    image_low = image_unit.astype(jnp.bfloat16)
    offsets = first_row + jnp.arange(rows, dtype=jnp.int32)
    label = (positive[0][:, None] == offsets[None, :]).astype(jnp.float32)
    text_grad, image_grad, sums = meeting(text_low, image_low, label, temp, shift)
    empty_label = jnp.zeros_like(label)
    visiting = text_low
    visiting = shifted(visiting, "dp", 1)
    text_term, image_term, more = meeting(visiting, image_low, empty_label, temp, shift)
    image_grad = image_grad + image_term
    sums = sums + more
    text_grad = text_grad + shifted(text_term.astype(jnp.bfloat16), "dp", -1).astype(
        text_term.dtype
    )
    own_text_grad = lax.psum_scatter(text_grad, "row", scatter_dimension=0, tiled=True)
    grad_text = unit_backward(own_text_grad, own_unit, own_inv)
    grad_image = unit_backward(image_grad, image_unit, image_inv)
    totals = lax.psum(sums, ("dp", "row"))
    count = block_rows * lax.axis_size("dp")
    loss = (totals[0] / count).reshape(1)
    grad_log_temp = (temp * totals[1] / count).reshape(1)
    grad_bias = (totals[2] / count).reshape(1)
    return (grad_text, grad_image, loss, grad_log_temp, grad_bias)


def solution(mesh):
    return jax.shard_map(
        on_device,
        mesh=mesh,
        in_specs=(P("dp", None), P(("dp", "row"), None), P("dp", None), P(), P()),
        out_specs=(P(("dp", "row"), None), P(("dp", "row"), None), P(), P(), P()),
        check_vma=False,
    )
```

profile of v0, /device:TPU:1, one launch (start us, length us, event | category | flops | bytes accessed | tf_op | source)
XLA Modules:
  0.0 376.4 jit_solution(5817737233435563471)
XLA Ops:
  7.2 0.0 reduce-scatter.2.cloned.1.call-start
  7.2 3.5 fusion
  10.7 0.3 copy-done
  11.0 4.6 %convert_multiply_fusion = (f32[2048,1152]{1,0:T(8,128)}, bf16[2048,1152]{1,0:T(8,128)(2,1)S(1)}) fusion(bf16[2048,1152]{1,0:T(8,128)(2,1)S(1)} %copy-done, f32[2048]{0:T(1024)S(1)} %add_rsqrt_fusion), kind=kLoop, calls=%fused_computation.2 | loop fusion | flops 7077888 | bytes 18882560 | tf_op jit(solution)/shard_map/mul | solution.py:15
  15.6 2.5 collective-permute-start
  19.4 0.3 fusion.13
  19.7 105.4 %collective-permute-done = bf16[2048,1152]{1,0:T(8,128)(2,1)S(1)} collective-permute-done((bf16[2048,1152]{1,0:T(8,128)(2,1)S(1)}, bf16[2048,1152]{1,0:T(8,128)(2,1)S(1)}, u32[]{:S(2)}, u32[]{:S(2)}) %collective-permute-start) | collective-permute-done | bytes 4718624 | tf_op jit(solution)/shard_map/ppermute | solution.py:9
  125.1 6.9 %fusion.5 = (f32[]{:T(128)}, f32[]{:T(128)}, f32[]{:T(128)}, f32[2048,512]{1,0:T(8,128)S(1)}) fusion(f32[]{:T(128)} %bitcast.16, f32[]{:T(128)} %bitcast, bf16[2048,1152]{1,0:T(8,128)(2,1)S(1)} %collective-permute-done, bf16[512,1152]{1,0:T(8,128)(2,1)S(1)} %copy-done.2, f32[512]{0:T(512)S(1)} %add_rsqrt_fusion.1), kind=kOutput, calls=%fused_computation.16 | convolution fusion | flops 2433417216 | bytes 10094612 | tf_op jit(solution)/shard_map/dot_general | solution.py:24
  132.0 5.4 %fusion.1 = bf16[2048,1152]{1,0:T(8,128)(2,1)} fusion(f32[]{:T(128)} %bitcast, bf16[512,1152]{1,0:T(8,128)(2,1)S(1)} %copy-done.2, f32[512]{0:T(512)S(1)} %add_rsqrt_fusion.1, f32[2048,512]{1,0:T(8,128)S(1)} %get-tuple-element.19, f32[]{:T(128)} %bitcast.18), kind=kOutput, calls=%fused_computation.8 | convolution fusion | flops 2428698624 | bytes 10094600 | tf_op jit(solution)/shard_map/dot_general | solution.py:32
  137.4 1.2 collective-permute-start.1
  138.6 9.6 %fusion.4 = (f32[]{:T(128)}, f32[]{:T(128)}, f32[]{:T(128)}, f32[2048,512]{1,0:T(8,128)S(1)}) fusion(s32[512]{0:T(512)S(1)} %iota_add_fusion, f32[]{:T(128)} %bitcast.17, f32[]{:T(128)} %bitcast, s32[2048]{0:T(1024)S(1)} %bitcast.21, bf16[2048,1152]{1,0:T(8,128)(2,1)} %copy-done.3, bf16[512,1152]{1,0:T(8,128)(2,1)S(1)} %copy-done.2, f32[512]{0:T(512)S(1)} %add_rsqrt_fusion.1), kind=kOutput, calls=%fused_computation.15 | convolution fusion | flops 2438660096 | bytes 10104852 | tf_op jit(solution)/shard_map/dot_general | solution.py:24
  148.2 91.6 %collective-permute-done.1 = bf16[2048,1152]{1,0:T(8,128)(2,1)} collective-permute-done((bf16[2048,1152]{1,0:T(8,128)(2,1)}, bf16[2048,1152]{1,0:T(8,128)(2,1)}, u32[]{:S(2)}, u32[]{:S(2)}) %collective-permute-start.1) | collective-permute-done | bytes 4718624 | tf_op jit(solution)/shard_map/ppermute | solution.py:9
  239.8 8.1 %convert_add_fusion = f32[2048,1152]{1,0:T(8,128)} fusion(bf16[2048,1152]{1,0:T(8,128)(2,1)} %collective-permute-done.1, f32[]{:T(128)} %bitcast, bf16[512,1152]{1,0:T(8,128)(2,1)S(1)} %copy-done.2, f32[512]{0:T(512)S(1)} %add_rsqrt_fusion.1, f32[2048,512]{1,0:T(8,128)S(1)} %get-tuple-element.18, s32[512]{0:T(512)S(1)} %iota_add_fusion, f32[]{:T(128)} %bitcast.15, ...), kind=kOutput, calls=%fused_computation.7 | convolution fusion | flops 2434203648 | bytes 19542024 | tf_op jit(solution)/shard_map/dot_general | solution.py:32
  247.9 0.0 reduce-scatter.2.cloned.1.call-update
  247.9 8.2 %fusion.16 = f32[512,1152]{1,0:T(8,128)} fusion(bf16[2048,1152]{1,0:T(8,128)(2,1)} %copy-done.3, f32[2048,512]{1,0:T(8,128)} %copy-done.6, s32[512]{0:T(512)S(1)} %iota_add_fusion, f32[]{:T(128)} %bitcast.20, f32[]{:T(128)} %bitcast, s32[2048]{0:T(1024)S(1)} %bitcast.23), kind=kOutput, calls=%fused_computation.37 | convolution fusion | flops 2425356288 | bytes 11282440 | tf_op jit(solution)/shard_map/dot_general | solution.py:33
  256.1 4.0 %maximum_add_fusion = f32[3]{0:T(128)S(1)} fusion(f32[1]{0:T(128)} %bitcast.5, f32[1]{0:T(128)} %bitcast.4, f32[1]{0:T(128)} %bitcast.3, f32[1]{0:T(128)} %bitcast.8, f32[1]{0:T(128)} %bitcast.7, f32[1]{0:T(128)} %bitcast.6), kind=kLoop, calls=%fused_computation.43 | loop fusion | flops 15 | bytes 36 | tf_op jit(solution)/shard_map/add | solution.py:60
  260.1 0.1 dynamic-slice.3
  260.2 87.4 %psum.7 = f32[3]{0:T(128)S(1)} all-reduce(f32[3]{0:T(128)S(1)} %maximum_add_fusion), channel_id=1, replica_groups=mesh['dp'=32,'row'=4] {'dp','row'}, use_global_device_ids=true, to_apply=%region_11.12 | all-reduce | flops 3 | bytes 24 | tf_op jit(solution)/shard_map/psum | solution.py:67
  347.6 0.6 fusion.28
  350.1 7.6 %fusion.10 = (f32[512]{0:T(512)S(1)}, f32[512,1152]{1,0:T(8,128)S(1)}) fusion(bf16[512,1152]{1,0:T(8,128)(2,1)S(1)} %copy-done.2, f32[512]{0:T(512)S(1)} %add_rsqrt_fusion.1, f32[]{:T(128)} %bitcast, f32[512,1152]{1,0:T(8,128)} %fusion.16, bf16[2048,1152]{1,0:T(8,128)(2,1)} %copy-done.4, f32[]{:T(128)} %bitcast.19, f32[2048,512]{1,0:T(8,128)} %copy-done.7), kind=kOutput, calls=%fused_computation.29 | convolution fusion | flops 2425748992 | bytes 14815240 | tf_op jit(solution)/shard_map/dot_general | solution.py:33
  357.7 1.9 fusion.12
  359.6 2.8 multiply_reduce_fusion.2
  362.4 0.3 copy-done.1
  362.7 3.4 subtract_multiply_fusion
  (18 shorter events, 0.0 us)
Async XLA Ops:
  7.2 352.4 %reduce-scatter.2.cloned.1.call-start = ((), (), s32[]{:S(2)}) async-start(), calls=%async_computation.1 | async-start | bytes 11796480 | tf_op jit(solution)/shard_map/reduce_scatter | solution.py:64
  7.2 3.8 copy-start
  11.0 8.5 %copy-start.2 = (bf16[512,1152]{1,0:T(8,128)(2,1)S(1)}, bf16[512,1152]{1,0:T(8,128)(2,1)}, u32[]{:S(2)}) copy-start(bf16[512,1152]{1,0:T(8,128)(2,1)} %param.6) | copy-start | bytes 3538948
  15.6 116.4 %copy-start.3 = (bf16[2048,1152]{1,0:T(8,128)(2,1)}, bf16[2048,1152]{1,0:T(8,128)(2,1)S(1)}, u32[]{:S(2)}) copy-start(bf16[2048,1152]{1,0:T(8,128)(2,1)S(1)} %get-tuple-element.12) | copy-start | bytes 14155780
  15.6 109.5 %collective-permute-start = (bf16[2048,1152]{1,0:T(8,128)(2,1)S(1)}, bf16[2048,1152]{1,0:T(8,128)(2,1)S(1)}, u32[]{:S(2)}, u32[]{:S(2)}) collective-permute-start(bf16[2048,1152]{1,0:T(8,128)(2,1)S(1)} %get-tuple-element.12), channel_id=1, source_target_pairs={{0,4},{4,8},{8,12},{12,16},{16,20},{20,24},{24,28},{28,32},{32,36}... | collective-permute-start | bytes 14155784 | tf_op jit(solution)/shard_map/ppermute | solution.py:9
  125.1 6.9 %copy-start.4 = (bf16[2048,1152]{1,0:T(8,128)(2,1)}, bf16[2048,1152]{1,0:T(8,128)(2,1)S(1)}, u32[]{:S(2)}) copy-start(bf16[2048,1152]{1,0:T(8,128)(2,1)S(1)} %collective-permute-done) | copy-start | bytes 14155780
  132.0 5.4 %copy-start.7 = (f32[2048,512]{1,0:T(8,128)}, f32[2048,512]{1,0:T(8,128)S(1)}, u32[]{:S(2)}) copy-start(f32[2048,512]{1,0:T(8,128)S(1)} %get-tuple-element.19) | copy-start | bytes 12582916
  132.0 6.5 %copy-start.5 = (s32[1,2048]{1,0:T(1,128)S(1)}, s32[1,2048]{1,0:T(1,128)}, u32[]{:S(2)}) copy-start(s32[1,2048]{1,0:T(1,128)} %param.7) | copy-start | bytes 24580
  137.4 102.4 %collective-permute-start.1 = (bf16[2048,1152]{1,0:T(8,128)(2,1)}, bf16[2048,1152]{1,0:T(8,128)(2,1)}, u32[]{:S(2)}, u32[]{:S(2)}) collective-permute-start(bf16[2048,1152]{1,0:T(8,128)(2,1)} %fusion.1), channel_id=1, source_target_pairs={{0,124},{4,0},{8,4},{12,8},{16,12},{20,16},{24,20},{28,24},{32,28}... | collective-permute-start | bytes 14155784 | tf_op jit(solution)/shard_map/ppermute | solution.py:9
  148.2 91.6 %copy-start.6 = (f32[2048,512]{1,0:T(8,128)}, f32[2048,512]{1,0:T(8,128)S(1)}, u32[]{:S(2)}) copy-start(f32[2048,512]{1,0:T(8,128)S(1)} %get-tuple-element.18) | copy-start | bytes 12582916
  359.6 3.1 copy-start.1
Sparse Core Ops, SparseCore 0:
  248.0 87.6 reduce-scatter.1
where the time goes:
time: 377 us; the launch traced here: 376 us
  waiting for transfers between devices  197 us (52%)
  blocking collectives  87.4 us (23%)
  matrix products  45.8 us (12%)
  between operations  20.8 us (6%)
  other arithmetic  20.6 us (5%)
    ppermute x2, waiting for transfers between devices, shifted(): return lax.ppermute(x, axis, [(i, (i + by) % count) for i in range(count)])  197 us
    psum x1, blocking collectives, on_device(): totals = lax.psum(sums, ('dp', 'row'))  87.4 us
    dot_general x2, matrix products, meeting(): lax.dot_general(text_low, image_low, (((1,), (1,)), ((), ())), preferred_...  16.5 us
    dot_general x2, matrix products, meeting(): lax.dot_general(slope_low, text_low, (((0,), (0,)), ((), ())), preferred_...  15.8 us
    dot_general x2, matrix products, meeting(): jnp.dot(slope_low, image_low, preferred_element_type=jnp.float32)  13.5 us
  transfers between devices with their start and end apart: 3, of which 2 were waited for; matrix products, arithmetic and copies ran while one was open for 9% of the time, Pallas kernels for 0%

commit v1 on v0

v1 whole, which is shorter than its diff:
```python
import functools

import jax
import jax.numpy as jnp
from jax import lax
from jax.experimental import pallas as pl
from jax.experimental.pallas import tpu as pltpu
from jax.sharding import PartitionSpec as P

MESH = pl.DeviceIdType.MESH
NT = (((1,), (1,)), ((), ()))

IMG, IMG_NEXT, TXT, TXT_PREV = 0, 4, 8, 12

(X_IMG, C_IMG, Z_IMG, Z_TXT_OPP, Z_TXT, Z_IMG_OPP, F_IMG, F_NEXT, F_NEXT_OPP, F_PREV_OPP, F_PREV) = range(11)


def kernel(n_dp, text, image, positive, log_temp, bias, grad_text, grad_image, out_sums,
           held, raw, cosines, slopes, pos_cols, sums, step_in, step_out,
           load_sem, raw_sem, send_sem, recv_sem, step_send, step_recv):
    _, parts, chunk, width = held.shape
    rows = parts * chunk
    n_steps = step_in.shape[0]
    dp, row = lax.axis_index("dp"), lax.axis_index("row")
    side = row + 1 - 2 * (row % 2)
    opposite = (row + 2) % 4
    quarter = (row, side, opposite, (side + 2) % 4)
    up, down = (dp + 1) % n_dp, (dp + n_dp - 1) % n_dp
    last_z, first_z = dp % 4 == 3, dp % 4 == 0

    def flipped(bit):
        return dp + bit - 2 * bit * ((dp // bit) % 2)

    partners = [(dp, side), (dp, opposite)]
    bit = 1
    while bit < n_dp:
        partners.append((flipped(bit), row))
        bit *= 2

    barrier = pltpu.get_barrier_semaphore()
    greeted = [(dp, side), (dp, opposite), (up, row), (up, opposite), (down, row), (down, opposite)] + partners[3:]
    for device in greeted:
        pl.semaphore_signal(barrier, inc=1, device_id=device, device_id_type=MESH)

    def load(source, first, slot, k, sem):
        return pltpu.make_async_copy(
            source.at[pl.ds(pl.multiple_of(first + k * chunk, chunk), chunk)], held.at[slot, k], sem)

    loads = {}
    for k in range(parts):
        loads[IMG, k] = load(image, 0, IMG, k, load_sem.at[0, k])
        loads[IMG, k].start()
    for j in (2, 0, 1, 3):
        for k in range(parts):
            loads[TXT + j, k] = load(text, quarter[j] * rows, TXT + j, k, load_sem.at[1 + j, k])
            loads[TXT + j, k].start()
    own_text = pltpu.make_async_copy(text.at[pl.ds(pl.multiple_of(row * rows, rows), rows)], raw.at[0], raw_sem.at[0])
    own_image = pltpu.make_async_copy(image, raw.at[1], raw_sem.at[1])
    own_text.start()
    own_image.start()

    temp = jnp.exp(jnp.full((8, 128), log_temp[0], jnp.float32))[0:1, 0:1]
    shift = bias[0]

    def normalise(slot, k):
        loads[slot, k].wait()
        for first in range(0, chunk, 64):
            block = pl.ds(first, min(64, chunk))
            full = held[slot, k, block].astype(jnp.float32)
            inverse = lax.rsqrt(jnp.sum(full * full, axis=-1, keepdims=True) + 1e-06)
            held[slot, k, block] = (full * inverse).astype(jnp.bfloat16)

    def copy(kind, k, source, target, device):
        return pltpu.make_async_remote_copy(
            src_ref=held.at[source, k], dst_ref=held.at[target, k],
            send_sem=send_sem.at[kind, k], recv_sem=recv_sem.at[kind, k],
            device_id=device, device_id_type=MESH)

    def x_img(k):
        return copy(X_IMG, k, IMG, IMG + 2, (dp, opposite))

    def c_img(k):
        return copy(C_IMG, k, IMG, IMG + 1, (dp, side))

    def z_img(k):
        return copy(Z_IMG, k, IMG, IMG_NEXT, (down, row))

    def z_img_opp(k):
        return copy(Z_IMG_OPP, k, jnp.where(first_z, IMG, IMG + 2), IMG_NEXT + 2,
                    (down, jnp.where(first_z, opposite, row)))

    def z_txt(k):
        return copy(Z_TXT, k, TXT, TXT_PREV, (up, row))

    def z_txt_opp(k):
        return copy(Z_TXT_OPP, k, jnp.where(last_z, TXT, TXT + 2), TXT_PREV + 2,
                    (up, jnp.where(last_z, opposite, row)))

    def forward(kind, slot):
        return lambda k: copy(kind, k, slot, slot + 1, (dp, side))

    f_img, f_next = forward(F_IMG, IMG + 2), forward(F_NEXT, IMG_NEXT)
    f_next_opp, f_prev_opp = forward(F_NEXT_OPP, IMG_NEXT + 2), forward(F_PREV_OPP, TXT_PREV + 2)
    f_prev = forward(F_PREV, TXT_PREV)

    for k in range(parts):
        normalise(IMG, k)
    pl.semaphore_wait(barrier, len(greeted))
    for k in range(parts):
        x_img(k).start()
        z_img(k).start()
        c_img(k).start()
    for k in range(parts):
        normalise(TXT, k)
        normalise(TXT + 2, k)
        z_txt_opp(k).start()
    for j in (1, 3):
        for k in range(parts):
            normalise(TXT + j, k)

    mine = positive[:, pl.ds(pl.multiple_of(row * rows, 128), rows)]
    pos_cols[...] = jnp.transpose(jnp.broadcast_to(mine, (128, rows)))
    sums[...] = jnp.zeros_like(sums)
    grad_text[...] = jnp.zeros_like(grad_text)
    grad_image[...] = jnp.zeros_like(grad_image)

    def meet(own, slot, k, total, label, with_sums):
        other = held[slot, k]
        cosines[...] = lax.dot_general(
            held[own].reshape(rows, width), other, NT, preferred_element_type=jnp.float32)
        step = min(64, rows)
        for first in range(0, rows, step):
            block = pl.ds(first, step)
            cosine = cosines[block]
            logits = temp * cosine + shift
            if label is not None:
                is_pair = label(first, step)
                logits = jnp.where(is_pair, -logits, logits)
            small = jnp.exp(-jnp.abs(logits))
            upper = 1.0 / (1.0 + small)
            slope = jnp.where(logits >= 0, upper, small * upper)
            if label is not None:
                slope = jnp.where(is_pair, -slope, slope)
            slopes[block] = slope.astype(jnp.bfloat16)
            if with_sums:
                pair_loss = jnp.maximum(logits, 0.0) + jnp.log1p(small)
                for i, value in enumerate((pair_loss, slope * cosine, slope)):
                    value = jnp.sum(value.reshape(step // 8, 8, chunk), axis=0)
                    for lane in range(0, chunk, 128):
                        sums[i * 8:(i + 1) * 8] += value[:, lane:lane + 128]
        total[...] += jnp.dot(slopes[...], other, preferred_element_type=jnp.float32)

    def text_meets(slot, k, base, with_sums=True):
        def label(first, step):
            at = base + k * chunk + lax.broadcasted_iota(jnp.int32, (step, chunk), 1)
            pos = pos_cols[pl.ds(first, step)]
            return jnp.concatenate([pos] * (chunk // 128), axis=1) == at
        meet(TXT, slot, k, grad_text, None if base is None else label, with_sums)

    def image_meets(slot, k, base, with_sums=False):
        if base is not None:
            pos = positive[:, pl.ds(pl.multiple_of(base + k * chunk, 128), chunk)]

        def label(first, step):
            at = row * rows + first + lax.broadcasted_iota(jnp.int32, (step, chunk), 0)
            return jnp.broadcast_to(pos, (step, chunk)) == at
        meet(IMG, slot, k, grad_image, None if base is None else label, with_sums)

    def loop(count, body):
        pl.loop(0, count)(body)

    def exchange(step):
        return pltpu.make_async_remote_copy(
            src_ref=step_out.at[step], dst_ref=step_in.at[step],
            send_sem=step_send.at[step], recv_sem=step_recv.at[step],
            device_id=partners[step], device_id_type=MESH)

    loop(parts, lambda k: text_meets(IMG, k, row * rows))
    for j in range(4):
        loop(parts, lambda k: image_meets(TXT + j, k, quarter[j] * rows))

    @pl.loop(0, parts)
    def _(k):
        c_img(k).wait_recv()
        text_meets(IMG + 1, k, side * rows)

    @pl.loop(0, parts)
    def _(k):
        x_img(k).wait_recv()
        f_img(k).start()
        z_img_opp(k).start()
        text_meets(IMG + 2, k, opposite * rows)
        z_img(k).wait_recv()
        f_next(k).start()
        z_txt_opp(k).wait_recv()
        f_prev_opp(k).start()
        z_txt_opp(k).wait_send()
        z_txt(k).start()
        text_meets(IMG_NEXT, k, None)
        image_meets(TXT_PREV + 2, k, None, True)
        f_img(k).wait_recv()
        text_meets(IMG + 3, k, quarter[3] * rows)
        f_next(k).wait_recv()
        text_meets(IMG_NEXT + 1, k, None)
        f_prev_opp(k).wait_recv()
        image_meets(TXT_PREV + 3, k, None, True)

    step_out[0] = sums[...]
    for step in range(n_steps):
        exchange(step).start()
        exchange(step).wait_recv()
        total = step_out[step] + step_in[step]
        if step + 1 < n_steps:
            step_out[step + 1] = total
    sums[...] = total

    @pl.loop(0, parts)
    def _(k):
        z_img_opp(k).wait_recv()
        f_next_opp(k).start()
        z_txt(k).wait_recv()
        f_prev(k).start()
        text_meets(IMG_NEXT + 2, k, None, False)
        image_meets(TXT_PREV, k, None)
        f_next_opp(k).wait_recv()
        text_meets(IMG_NEXT + 3, k, None, False)
        f_prev(k).wait_recv()
        image_meets(TXT_PREV + 1, k, None)

    own_text.wait()
    own_image.wait()
    for total, which in ((grad_text, 0), (grad_image, 1)):
        @pl.loop(0, rows // 32)
        def _(i):
            block = pl.ds(pl.multiple_of(i * 32, 32), 32)
            full = raw[which, block].astype(jnp.float32)
            inverse = lax.rsqrt(jnp.sum(full * full, axis=-1, keepdims=True) + 1e-06)
            unit = full * inverse
            grad = temp * total[block]
            along = jnp.sum(unit * grad, axis=-1, keepdims=True)
            total[block] = (grad - unit * along) * inverse

    count = rows * 4 * n_dp
    out_sums[0] = jnp.sum(sums[0:8]) / count
    out_sums[1] = jnp.sum(temp * sums[8:16]) / count
    out_sums[2] = jnp.sum(sums[16:24]) / count

    @pl.loop(0, parts)
    def _(k):
        for made in (x_img, c_img, z_img, z_img_opp, z_txt, f_img, f_next, f_next_opp, f_prev_opp, f_prev):
            made(k).wait_send()
    for step in range(n_steps):
        exchange(step).wait_send()


def on_device(n_dp, text, image, positive, log_temp, bias):
    rows, width = image.shape
    chunk = min(256, rows // 2)
    parts = rows // chunk
    n_steps = 2 + (n_dp - 1).bit_length()
    vmem, smem, hbm = (pl.BlockSpec(memory_space=m) for m in (pltpu.VMEM, pltpu.SMEM, pl.ANY))
    dma = pltpu.SemaphoreType.DMA
    grad_text, grad_image, totals = pl.pallas_call(
        functools.partial(kernel, n_dp),
        out_shape=(
            jax.ShapeDtypeStruct((rows, width), jnp.float32),
            jax.ShapeDtypeStruct((rows, width), jnp.float32),
            jax.ShapeDtypeStruct((3,), jnp.float32),
        ),
        in_specs=[hbm, hbm, vmem, smem, smem],
        out_specs=(vmem, vmem, smem),
        scratch_shapes=[
            pltpu.VMEM((16, parts, chunk, width), jnp.bfloat16),
            pltpu.VMEM((2, rows, width), jnp.bfloat16),
            pltpu.VMEM((rows, chunk), jnp.float32),
            pltpu.VMEM((rows, chunk), jnp.bfloat16),
            pltpu.VMEM((rows, 128), jnp.int32),
            pltpu.VMEM((24, 128), jnp.float32),
            pltpu.VMEM((n_steps, 24, 128), jnp.float32),
            pltpu.VMEM((n_steps, 24, 128), jnp.float32),
            dma((5, parts)), dma((2,)), dma((11, parts)), dma((11, parts)), dma((n_steps,)), dma((n_steps,)),
        ],
        compiler_params=pltpu.CompilerParams(
            collective_id=0, has_side_effects=True, vmem_limit_bytes=48 * 1024 * 1024),
        cost_estimate=pl.CostEstimate(
            flops=2 * 32 * rows * rows * width, bytes_accessed=7 * rows * width * 2 + 2 * rows * width * 4,
            transcendentals=24 * rows * rows),
    )(text, image, positive, log_temp, bias)
    return grad_text, grad_image, totals[0:1], totals[1:2], totals[2:3]


def solution(mesh):
    return jax.shard_map(
        functools.partial(on_device, mesh.shape["dp"]),
        mesh=mesh,
        in_specs=(P("dp", None), P(("dp", "row"), None), P("dp", None), P(), P()),
        out_specs=(P(("dp", "row"), None), P(("dp", "row"), None), P(), P(), P()),
        check_vma=False,
    )
```

time: 377 us -> 136 us (0.36)
  waiting for transfers between devices: 197 us -> 0 us
  Pallas kernels: 0 us -> 128 us
  blocking collectives: 87.4 us -> 0 us
  matrix products: 45.8 us -> 0 us
  other arithmetic: 20.6 us -> 0 us
  between operations: 20.8 us -> 1.94 us
  local copies, waits for them, and re-layouts: 1.22 us -> 5.36 us
    ppermute x2 -> x0, waiting for transfers between devices: 197 us -> none  [shifted(): return lax.ppermute(x, axis, [(i, (i + by) % count) for i in range(count)])]
    pallas_call x0 -> x1, Pallas kernels: none -> 128 us  [on_device(): pl.pallas_call(functools.partial(kernel, n_dp), out_shape=(jax.ShapeDtype...]
    psum x1 -> x0, blocking collectives: 87.4 us -> none  [on_device(): totals = lax.psum(sums, ('dp', 'row'))]
    dot_general x6 -> x0, matrix products: 45.8 us -> none  [the longest x2 16.5 us: meeting(): lax.dot_general(text_low, image_low, (((1,), (1,)), ((), ())), preferred_...]
    mul x3 -> x0, other arithmetic: 9.95 us -> none  [the longest x2 5.32 us: unit_backward(): return (grad_unit - unit * along) * inverse]
    reduce_sum x3 -> x0, other arithmetic: 6.59 us -> none  [the longest x2 3.78 us: unit_rows(): inverse = lax.rsqrt(jnp.sum(full * full, axis=-1, keepdims=True) + 1e-06)]
    unnamed x16 -> x6, local copies, waits for them, and re-layouts: 0.55 us -> 4.77 us
    add x2 -> x0, other arithmetic: 4.01 us -> none  [the longest x1 4.01 us: on_device(): sums = sums + more]
  transfers between devices with their start and end apart: 3 -> 0, of which waited for: 2 -> 0; matrix products, arithmetic and copies ran while one was open for 9% -> 0% of each run, Pallas kernels for 0% -> 0%
where the time goes in v1:
time: 136 us
  Pallas kernels  128 us (94%)
  local copies, waits for them, and re-layouts  5.36 us (4%)
  between operations  1.94 us (1%)
    pallas_call x1, Pallas kernels, on_device(): pl.pallas_call(functools.partial(kernel, n_dp), out_shape=(jax.ShapeDtype...  128 us
    unnamed x6, local copies, waits for them, and re-layouts  4.77 us

profile of v1, /device:TPU:1, one launch (start us, length us, event | category | flops | bytes accessed | tf_op | source)
XLA Modules:
  0.0 135.5 jit_solution(11278815557830890896)
XLA Ops:
  1.9 0.0 copy-start
  1.9 1.3 copy-done
  3.2 0.0 copy-start.1
  3.2 0.7 copy-done.1
  3.9 128.2 %shard_map.92 = (f32[512,1152]{1,0:T(8,128)S(1)}, f32[512,1152]{1,0:T(8,128)S(1)}, f32[3]{0:T(128)S(1)}) custom-call(bf16[2048,1152]{1,0:T(8,128)(2,1)} %text.1, bf16[512,1152]{1,0:T(8,128)(2,1)S(1)} %copy-done, s32[1,2048]{1,0:T(1,128)S(1)} %copy-done.1, f32[1]{0:T(128)S(6)} %copy.12.log_temp, f32[1]{0:T(128)S(6)} %copy.13.bias), custom_call_target="tpu_custom_call" | custom-call | flops 19327352832 | bytes 12976128 | tf_op jit(solution)/shard_map/pallas_call | solution.py:263
  132.1 0.6 fusion
  132.7 1.4 %copy.14 = f32[512,1152]{1,0:T(8,128)} copy(f32[512,1152]{1,0:T(8,128)S(1)} %get-tuple-element.19) | data formatting | bytes 4718592
  134.1 1.4 %copy.15 = f32[512,1152]{1,0:T(8,128)} copy(f32[512,1152]{1,0:T(8,128)S(1)} %get-tuple-element.20) | data formatting | bytes 4718592
Async XLA Ops:
  1.9 1.3 copy-start
  3.2 0.7 copy-start.1

commit v2 on v0

v2 whole, which is shorter than its diff:
```python
import functools

import jax
import jax.numpy as jnp
from jax import lax
from jax.experimental import pallas as pl
from jax.experimental.pallas import tpu as pltpu
from jax.sharding import PartitionSpec as P

MESH = pl.DeviceIdType.MESH
NT = (((1,), (1,)), ((), ()))
LANES = 128

IMG, NEXT, TXT, PREV = range(4)

X_IMG, C_IMG, F_IMG, Z_IMG, F_NEXT, Z_TXT, F_PREV = 0, 1, 2, 3, 5, 7, 9
KINDS = 11
FOR_SIDE = 11
X_NEXT = 14


def kernel(n_dp, text, image, positive, log_temp, bias, grad_text, grad_image, out_sums,
           held, raw, cosines, slopes, pos, pos_cols, pos_rows, sums, met_a, met_b,
           load_sem, raw_sem, send_sem, recv_sem, send_a, recv_a, send_b, recv_b):
    parts, width = held.shape[2], held.shape[-1]
    rows = parts * LANES
    dp, row = lax.axis_index("dp"), lax.axis_index("row")
    side = row + 1 - 2 * (row % 2)
    opposite = (row + 2) % 4
    quarter = ((row, side), (opposite, (side + 2) % 4))
    up, down = (dp + 1) % n_dp, (dp + n_dp - 1) % n_dp
    first_z, last_z = dp % 4 == 0, dp % 4 == 3
    end_z = jnp.logical_or(first_z, last_z)
    before_last_z = dp % 4 == 2
    core0, core1 = row % 2 == 0, row % 2 == 1
    opposite_side = quarter[1][1]

    n_b = met_b.shape[0]
    n_y = n_dp // n_b
    y, rest = dp // n_b, dp % n_b
    place_a = y * 4 + row
    group_a = [(((y + i // 4) % n_y) * n_b + rest, (row + i % 4) % 4) for i in range(1, 4 * n_y)]
    group_b = [(y * n_b + (rest + i) % n_b, row) for i in range(1, n_b)]

    barrier = pltpu.get_barrier_semaphore()
    greeted = [(near, (row + i) % 4) for near in (up, down) for i in range(4)] + group_a + group_b
    for device in greeted:
        pl.semaphore_signal(barrier, inc=1, device_id=device, device_id_type=MESH)

    def load(source, first, group, pair, k, core):
        first = pl.multiple_of(first + k * LANES, LANES)
        return pltpu.make_async_copy(source.at[pl.ds(first, LANES)], held.at[group, pair, k, core],
                                     load_sem.at[0 if group == IMG else 1 + 2 * pair + core, k])

    def load_image(k):
        return load(image, 0, IMG, 0, k, 0)

    def load_text(pair, core, k):
        return load(text, quarter[pair][core] * rows, TXT, pair, k, core)

    for k in range(parts):
        load_image(k).start()
    pos_copy = pltpu.make_async_copy(positive, pos, raw_sem.at[2])
    for pair, core in ((0, 0), (1, 0), (0, 1), (1, 1)):
        for k in range(parts):
            load_text(pair, core, k).start()
        if core == 0 and pair == 1:
            pos_copy.start()
    own_text = pltpu.make_async_copy(text.at[pl.ds(pl.multiple_of(row * rows, rows), rows)], raw.at[0], raw_sem.at[0])
    own_image = pltpu.make_async_copy(image, raw.at[1], raw_sem.at[1])
    own_text.start()
    own_image.start()

    temp = jnp.exp(jnp.full((8, LANES), log_temp[0], jnp.float32))[0:1, 0:1]
    shift = bias[0]

    def normalise(group, pair, k, core):
        full = held[group, pair, k, core].astype(jnp.float32)
        inverse = lax.rsqrt(jnp.sum(full * full, axis=-1, keepdims=True) + 1e-06)
        held[group, pair, k, core] = (full * inverse).astype(jnp.bfloat16)

    def copy(kind, k, source, target, device, sent=None):
        return pltpu.make_async_remote_copy(
            src_ref=held.at[source], dst_ref=held.at[target],
            send_sem=send_sem.at[kind if sent is None else sent, k], recv_sem=recv_sem.at[kind, k],
            device_id=device, device_id_type=MESH)

    def x_img(k):
        return copy(X_IMG, k, (IMG, 0, k, 0), (IMG, 1, k, 0), (dp, opposite))

    def x_img_for_side(k):
        return copy(X_IMG, k, (IMG, 0, k, 1), (IMG, 1, k, 0), (dp, opposite_side), FOR_SIDE)

    def c_img(k):
        return copy(C_IMG, k, (IMG, 0, k, 0), (IMG, 0, k, 1), (dp, side))

    def f_img(k):
        return copy(F_IMG, k, (IMG, 1, k, 0), (IMG, 1, k, 1), (dp, side))

    def z_img(pair, k):
        across = jnp.logical_and(first_z, pair == 1)
        return copy(Z_IMG + pair, k, (IMG, jnp.where(across, 0, pair), k, 0), (NEXT, pair, k, 0),
                    (down, jnp.where(across, opposite, row)))

    def x_next(k):
        return copy(Z_IMG + 1, k, (NEXT, 0, k, 0), (NEXT, 1, k, 0), (dp, opposite), X_NEXT)

    def z_img_for_side(pair, k):
        return copy(Z_IMG + pair, k, (IMG, 0, k, 1), (NEXT, pair, k, 0),
                    (down, opposite_side if pair else side), FOR_SIDE + 1 + pair)

    def z_txt(pair, k):
        across = jnp.logical_and(last_z, pair == 1)
        return copy(Z_TXT + pair, k, (TXT, jnp.where(across, 0, pair), k, 0), (PREV, pair, k, 0),
                    (up, jnp.where(across, opposite, row)))

    def z_txt_for_side(pair, k):
        return copy(Z_TXT + pair, k, (TXT, 0, k, 1), (PREV, pair, k, 0),
                    (up, opposite_side if pair else side), FOR_SIDE + 1 + pair)

    def f_next(pair, k):
        return copy(F_NEXT + pair, k, (NEXT, pair, k, 0), (NEXT, pair, k, 1), (dp, side))

    def f_prev(pair, k):
        return copy(F_PREV + pair, k, (PREV, pair, k, 0), (PREV, pair, k, 1), (dp, side))

    sends_x = jnp.logical_or(jnp.logical_not(end_z), core1)
    sends_img = jnp.logical_or(jnp.logical_not(first_z), core0)
    sends_txt = jnp.logical_or(jnp.logical_not(last_z), core0)
    img_for_side = jnp.logical_and(first_z, core0)
    txt_for_side = jnp.logical_and(last_z, core0)
    x_for_side = jnp.logical_and(end_z, core1)

    for k in range(parts):
        load_image(k).wait()
        normalise(IMG, 0, k, 0)
        if k == 0:
            pl.semaphore_wait(barrier, len(greeted))
        c_img(k).start()

        @pl.when(jnp.logical_not(end_z))
        def _():
            x_img(k).start()
            z_img(0, k).start()

    for k in range(parts):
        c_img(k).wait_recv()

        @pl.when(jnp.logical_and(end_z, core1))
        def _():
            x_img(k).start()
            x_img_for_side(k).start()

        @pl.when(last_z)
        def _():
            z_img(0, k).start()

        @pl.when(img_for_side)
        def _():
            z_img(0, k).start()
            z_img(1, k).start()
            z_img_for_side(0, k).start()
            z_img_for_side(1, k).start()

    for k in range(parts):
        load_text(0, 0, k).wait()
        normalise(TXT, 0, k, 0)

        @pl.when(sends_txt)
        def _():
            z_txt(0, k).start()

        load_text(0, 1, k).wait()
        normalise(TXT, 0, k, 1)

        @pl.when(txt_for_side)
        def _():
            z_txt(1, k).start()
            z_txt_for_side(0, k).start()
            z_txt_for_side(1, k).start()

    for k in range(parts):
        load_text(1, 0, k).wait()
        normalise(TXT, 1, k, 0)

        @pl.when(jnp.logical_not(last_z))
        def _():
            z_txt(1, k).start()

    for k in range(parts):
        load_text(1, 1, k).wait()
        normalise(TXT, 1, k, 1)

    pos_copy.wait()
    mine = pos[:, pl.ds(pl.multiple_of(row * rows, LANES), rows)]
    pos_cols[...] = jnp.transpose(jnp.broadcast_to(mine, (LANES, rows)))
    for pair in range(2):
        for k in range(parts):
            for core in range(2):
                at = pl.multiple_of(quarter[pair][core] * rows + k * LANES, LANES)
                pos_rows[pair, :, pl.ds((2 * k + core) * LANES, LANES)] = pos[:, pl.ds(at, LANES)]
    sums[...] = jnp.zeros_like(sums)

    span = 2 * LANES
    step = 64

    def meet(own, group, pair, k0, count, total, label, with_sums, fresh=False):
        mine = held[own, 0, :, 0].reshape(rows, width)
        for i in range(count):
            other = held[group, pair, k0 + i].reshape(span, width)
            here = cosines.at[i % 2]
            here[...] = lax.dot_general(mine, other, NT, preferred_element_type=jnp.float32)
            for first in range(0, rows, step):
                block = pl.ds(first, step)
                cosine = here[block]
                logits = temp * cosine + shift
                if label is not None:
                    is_pair = label(first, k0 + i)
                    logits = jnp.where(is_pair, -logits, logits)
                small = jnp.exp(-jnp.abs(logits))
                upper = 1.0 / (1.0 + small)
                slope = jnp.where(logits >= 0, upper, small * upper)
                if label is not None:
                    slope = jnp.where(is_pair, -slope, slope)
                slopes[block, i * span:(i + 1) * span] = slope.astype(jnp.bfloat16)
                if with_sums:
                    pair_loss = jnp.maximum(logits, 0.0) + jnp.log1p(small)
                    for j, value in enumerate((pair_loss, slope * cosine, slope)):
                        value = jnp.sum(value.reshape(step // 8, 8, span), axis=0)
                        sums[j * 8:(j + 1) * 8] += value[:, :LANES] + value[:, LANES:]
        product = jnp.dot(slopes[:, :count * span], held[group, pair, pl.ds(k0, count)].reshape(count * span, width),
                          preferred_element_type=jnp.float32)
        total[...] = product if fresh else total[...] + product

    def text_meets_own(pair, k0, count, fresh=False):
        def label(first, k):
            lane = lax.broadcasted_iota(jnp.int32, (step, LANES), 1) + k * LANES
            at = jnp.concatenate([lane + quarter[pair][core] * rows for core in range(2)], axis=1)
            here = pos_cols[pl.ds(first, step)]
            return jnp.concatenate([here, here], axis=1) == at
        meet(TXT, IMG, pair, k0, count, grad_text, label, True, fresh)

    def image_meets_own(pair, fresh=False):
        def label(first, k):
            at = lax.broadcasted_iota(jnp.int32, (step, span), 0) + (row * rows + first)
            return jnp.broadcast_to(pos_rows[pair, :, pl.ds(k * span, span)], (step, span)) == at
        meet(IMG, TXT, pair, 0, parts, grad_image, label, False, fresh)

    image_meets_own(0, True)
    text_meets_own(0, 0, parts, True)
    image_meets_own(1)

    def to_a(i):
        return pltpu.make_async_remote_copy(
            src_ref=sums, dst_ref=met_a.at[place_a], send_sem=send_a.at[i], recv_sem=recv_a.at[i],
            device_id=group_a[i], device_id_type=MESH)

    def to_b(i):
        return pltpu.make_async_remote_copy(
            src_ref=met_b.at[rest], dst_ref=met_b.at[rest], send_sem=send_b.at[i], recv_sem=recv_b.at[i],
            device_id=group_b[i], device_id_type=MESH)

    @pl.loop(0, 2 * parts)
    def _(s):
        next_pair, next_k = jnp.where(last_z, s % 2, s // parts), jnp.where(last_z, s // 2, s % parts)
        prev_pair, prev_k = jnp.where(first_z, s % 2, s // parts), jnp.where(first_z, s // 2, s % parts)
        x_now = jnp.where(end_z, s % 2, 1 - s // parts) == 1
        x_k = jnp.where(end_z, s // 2, s % parts)

        @pl.when(x_now)
        def _():
            x_img(x_k).wait_recv()
            f_img(x_k).start()

            @pl.when(jnp.logical_not(end_z))
            def _():
                z_img(1, x_k).start()

        z_img(next_pair, next_k).wait_recv()
        f_next(next_pair, next_k).start()

        @pl.when(jnp.logical_and(before_last_z, s < parts))
        def _():
            x_next(next_k).start()

        z_txt(prev_pair, prev_k).wait_recv()
        f_prev(prev_pair, prev_k).start()
        f_next(next_pair, next_k).wait_recv()
        meet(TXT, NEXT, next_pair, next_k, 1, grad_text, None, True)

        @pl.when(x_now)
        def _():
            f_img(x_k).wait_recv()
            text_meets_own(1, x_k, 1)

        @pl.when(s == 2 * parts - 1)
        def _():
            for i in range(len(group_a)):
                to_a(i).start()
            met_a[place_a] = sums[...]

        f_prev(prev_pair, prev_k).wait_recv()
        meet(IMG, PREV, prev_pair, prev_k, 1, grad_image, None, False)

    for i in range(len(group_a)):
        to_a(i).wait_recv()
    met_b[rest] = functools.reduce(lambda a, b: a + b, [met_a[i] for i in range(4 * n_y)])
    for i in range(len(group_b)):
        to_b(i).start()

    own_text.wait()
    own_image.wait()
    for total, which in ((grad_text, 0), (grad_image, 1)):
        @pl.loop(0, parts)
        def _(k):
            block = pl.ds(pl.multiple_of(k * LANES, LANES), LANES)
            full = raw[which, block].astype(jnp.float32)
            grad = temp * total[block]
            inverse = lax.rsqrt(jnp.sum(full * full, axis=-1, keepdims=True) + 1e-06)
            unit = full * inverse
            along = jnp.sum(unit * grad, axis=-1, keepdims=True)
            total[block] = (grad - unit * along) * inverse

    for i in range(len(group_b)):
        to_b(i).wait_recv()
    total = functools.reduce(lambda a, b: a + b, [met_b[i] for i in range(n_b)])
    count = rows * 4 * n_dp
    out_sums[0] = jnp.sum(total[0:8]) / count
    out_sums[1] = jnp.sum(temp * total[8:16]) / count
    out_sums[2] = jnp.sum(total[16:24]) / count

    @pl.loop(0, parts)
    def _(k):
        for made in (c_img, f_img):
            made(k).wait_send()
        for pair in range(2):
            for made in (f_next, f_prev):
                made(pair, k).wait_send()

        @pl.when(sends_x)
        def _():
            x_img(k).wait_send()

        @pl.when(x_for_side)
        def _():
            x_img_for_side(k).wait_send()

        @pl.when(before_last_z)
        def _():
            x_next(k).wait_send()

        for sends, for_side, made, made_for_side in (
                (sends_img, img_for_side, z_img, z_img_for_side), (sends_txt, txt_for_side, z_txt, z_txt_for_side)):
            @pl.when(sends)
            def _():
                made(0, k).wait_send()

            @pl.when(jnp.logical_and(sends, jnp.logical_not(last_z)) if made is z_img else sends)
            def _():
                made(1, k).wait_send()

            @pl.when(for_side)
            def _():
                for pair in range(2):
                    made_for_side(pair, k).wait_send()

    for i in range(len(group_a)):
        to_a(i).wait_send()
    for i in range(len(group_b)):
        to_b(i).wait_send()


def on_device(n_dp, text, image, positive, log_temp, bias):
    rows, width = image.shape
    parts = rows // LANES
    n_b = min(n_dp, 8)
    n_a = 4 * (n_dp // n_b)
    vmem, smem, hbm = (pl.BlockSpec(memory_space=m) for m in (pltpu.VMEM, pltpu.SMEM, pltpu.HBM))
    dma = pltpu.SemaphoreType.DMA
    grad_text, grad_image, totals = pl.pallas_call(
        functools.partial(kernel, n_dp),
        out_shape=(
            jax.ShapeDtypeStruct((rows, width), jnp.float32),
            jax.ShapeDtypeStruct((rows, width), jnp.float32),
            jax.ShapeDtypeStruct((3,), jnp.float32),
        ),
        in_specs=[hbm, hbm, hbm, smem, smem],
        out_specs=(vmem, vmem, smem),
        scratch_shapes=[
            pltpu.VMEM((4, 2, parts, 2, LANES, width), jnp.bfloat16),
            pltpu.VMEM((2, rows, width), jnp.bfloat16),
            pltpu.VMEM((2, rows, 2 * LANES), jnp.float32),
            pltpu.VMEM((rows, 2 * rows), jnp.bfloat16),
            pltpu.VMEM((1, 4 * rows), jnp.int32),
            pltpu.VMEM((rows, LANES), jnp.int32),
            pltpu.VMEM((2, 1, 2 * rows), jnp.int32),
            pltpu.VMEM((24, LANES), jnp.float32),
            pltpu.VMEM((n_a, 24, LANES), jnp.float32),
            pltpu.VMEM((n_b, 24, LANES), jnp.float32),
            dma((5, parts)), dma((3,)), dma((KINDS + 4, parts)), dma((KINDS, parts)),
            dma((n_a,)), dma((n_a,)), dma((n_b,)), dma((n_b,)),
        ],
        compiler_params=pltpu.CompilerParams(
            collective_id=0, has_side_effects=True, vmem_limit_bytes=48 * 1024 * 1024),
        cost_estimate=pl.CostEstimate(
            flops=2 * 32 * rows * rows * width, bytes_accessed=7 * rows * width * 2 + 2 * rows * width * 4,
            transcendentals=24 * rows * rows),
    )(text, image, positive, log_temp, bias)
    return grad_text, grad_image, totals[0:1], totals[1:2], totals[2:3]


def solution(mesh):
    return jax.shard_map(
        functools.partial(on_device, mesh.shape["dp"]),
        mesh=mesh,
        in_specs=(P("dp", None), P(("dp", "row"), None), P("dp", None), P(), P()),
        out_specs=(P(("dp", "row"), None), P(("dp", "row"), None), P(), P(), P()),
        check_vma=False,
    )
```

time: 377 us -> 93.2 us (0.25)
  waiting for transfers between devices: 197 us -> 0 us
  blocking collectives: 87.4 us -> 0 us
  Pallas kernels: 0 us -> 85.7 us
  matrix products: 45.8 us -> 0 us
  other arithmetic: 20.6 us -> 0 us
  between operations: 20.8 us -> 1.94 us
  local copies, waits for them, and re-layouts: 1.22 us -> 5.36 us
    ppermute x2 -> x0, waiting for transfers between devices: 197 us -> none  [shifted(): return lax.ppermute(x, axis, [(i, (i + by) % count) for i in range(count)])]
    psum x1 -> x0, blocking collectives: 87.4 us -> none  [on_device(): totals = lax.psum(sums, ('dp', 'row'))]
    pallas_call x0 -> x1, Pallas kernels: none -> 85.7 us  [on_device(): pl.pallas_call(functools.partial(kernel, n_dp), out_shape=(jax.ShapeDtype...]
    dot_general x6 -> x0, matrix products: 45.8 us -> none  [the longest x2 16.5 us: meeting(): lax.dot_general(text_low, image_low, (((1,), (1,)), ((), ())), preferred_...]
    mul x3 -> x0, other arithmetic: 9.95 us -> none  [the longest x2 5.32 us: unit_backward(): return (grad_unit - unit * along) * inverse]
    reduce_sum x3 -> x0, other arithmetic: 6.59 us -> none  [the longest x2 3.78 us: unit_rows(): inverse = lax.rsqrt(jnp.sum(full * full, axis=-1, keepdims=True) + 1e-06)]
    unnamed x16 -> x6, local copies, waits for them, and re-layouts: 0.55 us -> 4.77 us
    add x2 -> x0, other arithmetic: 4.01 us -> none  [the longest x1 4.01 us: on_device(): sums = sums + more]
  transfers between devices with their start and end apart: 3 -> 0, of which waited for: 2 -> 0; matrix products, arithmetic and copies ran while one was open for 9% -> 0% of each run, Pallas kernels for 0% -> 0%
where the time goes in v2:
time: 93.2 us; the launch traced here: 93 us
  Pallas kernels  85.7 us (92%)
  local copies, waits for them, and re-layouts  5.36 us (6%)
  between operations  1.94 us (2%)
    pallas_call x1, Pallas kernels, on_device(): pl.pallas_call(functools.partial(kernel, n_dp), out_shape=(jax.ShapeDtype...  85.7 us
    unnamed x6, local copies, waits for them, and re-layouts  4.77 us

profile of v2, /device:TPU:1, one launch (start us, length us, event | category | flops | bytes accessed | tf_op | source)
XLA Modules:
  0.0 93.0 jit_solution(17726194136810827421)
XLA Ops:
  1.9 0.0 copy-start
  1.9 1.3 %copy-done = bf16[512,1152]{1,0:T(8,128)(2,1)S(1)} copy-done((bf16[512,1152]{1,0:T(8,128)(2,1)S(1)}, bf16[512,1152]{1,0:T(8,128)(2,1)}, u32[]{:S(2)}) %copy-start) | copy-done | bytes 1179672
  3.2 0.0 copy-start.1
  3.2 0.7 copy-done.1
  3.9 85.7 %shard_map.92 = (f32[512,1152]{1,0:T(8,128)S(1)}, f32[512,1152]{1,0:T(8,128)S(1)}, f32[3]{0:T(128)S(1)}) custom-call(bf16[2048,1152]{1,0:T(8,128)(2,1)} %text.1, bf16[512,1152]{1,0:T(8,128)(2,1)S(1)} %copy-done, s32[1,2048]{1,0:T(1,128)S(1)} %copy-done.1, f32[1]{0:T(128)S(6)} %copy.12.log_temp, f32[1]{0:T(128)S(6)} %copy.13.bias), custom_call_target="tpu_custom_call" | custom-call | flops 19327352832 | bytes 12976128 | tf_op jit(solution)/shard_map/pallas_call | solution.py:380
  89.6 0.6 fusion
  90.2 1.4 %copy.14 = f32[512,1152]{1,0:T(8,128)} copy(f32[512,1152]{1,0:T(8,128)S(1)} %get-tuple-element.19) | data formatting | bytes 4718592
  91.6 1.4 %copy.15 = f32[512,1152]{1,0:T(8,128)} copy(f32[512,1152]{1,0:T(8,128)S(1)} %get-tuple-element.20) | data formatting | bytes 4718592
Async XLA Ops:
  1.9 1.3 %copy-start = (bf16[512,1152]{1,0:T(8,128)(2,1)S(1)}, bf16[512,1152]{1,0:T(8,128)(2,1)}, u32[]{:S(2)}) copy-start(bf16[512,1152]{1,0:T(8,128)(2,1)} %image.1) | copy-start | bytes 3538948
  3.2 0.7 copy-start.1

commit v3 on v2

--- a/solution.py
+++ b/solution.py
@@ -20,7 +20,7 @@
 
 
 def kernel(n_dp, text, image, positive, log_temp, bias, grad_text, grad_image, out_sums,
-           held, raw, cosines, slopes, pos, pos_cols, pos_rows, sums, met_a, met_b,
+           held, raw, inverses, cosines, slopes, pos, pos_cols, pos_rows, sums, packed, met_a, met_b,
            load_sem, raw_sem, send_sem, recv_sem, send_a, recv_a, send_b, recv_b):
     parts, width = held.shape[2], held.shape[-1]
     rows = parts * LANES
@@ -78,11 +78,13 @@
         full = held[group, pair, k, core].astype(jnp.float32)
         inverse = lax.rsqrt(jnp.sum(full * full, axis=-1, keepdims=True) + 1e-06)
         held[group, pair, k, core] = (full * inverse).astype(jnp.bfloat16)
+        if pair == 0 and core == 0:
+            inverses[0 if group == TXT else 1, k] = jnp.broadcast_to(inverse, (LANES, LANES))
 
     def copy(kind, k, source, target, device, sent=None):
         return pltpu.make_async_remote_copy(
             src_ref=held.at[source], dst_ref=held.at[target],
-            send_sem=send_sem.at[kind if sent is None else sent, k], recv_sem=recv_sem.at[kind, k],
+            send_sem=send_sem.at[kind if sent is None else sent], recv_sem=recv_sem.at[kind, k],
             device_id=device, device_id_type=MESH)
 
     def x_img(k):
@@ -141,26 +143,20 @@
         @pl.when(jnp.logical_not(end_z))
         def _():
             x_img(k).start()
+
+        @pl.when(jnp.logical_not(first_z))
+        def _():
             z_img(0, k).start()
 
-    for k in range(parts):
-        c_img(k).wait_recv()
-
-        @pl.when(jnp.logical_and(end_z, core1))
-        def _():
-            x_img(k).start()
-            x_img_for_side(k).start()
-
-        @pl.when(last_z)
-        def _():
-            z_img(0, k).start()
-
-        @pl.when(img_for_side)
-        def _():
-            z_img(0, k).start()
-            z_img(1, k).start()
-            z_img_for_side(0, k).start()
-            z_img_for_side(1, k).start()
+        if k == 0:
+            @pl.when(img_for_side)
+            def _():
+                z_img(0, k).start()
+                z_img(1, k).start()
+
+            @pl.when(x_for_side)
+            def _():
+                x_img(k).start()
 
     for k in range(parts):
         load_text(0, 0, k).wait()
@@ -178,6 +174,22 @@
             z_txt(1, k).start()
             z_txt_for_side(0, k).start()
             z_txt_for_side(1, k).start()
+
+        c_img(k).wait_recv()
+
+        @pl.when(x_for_side)
+        def _():
+            x_img_for_side(k).start()
+            if k + 1 < parts:
+                x_img(k + 1).start()
+
+        @pl.when(img_for_side)
+        def _():
+            z_img_for_side(0, k).start()
+            z_img_for_side(1, k).start()
+            if k + 1 < parts:
+                z_img(0, k + 1).start()
+                z_img(1, k + 1).start()
 
     for k in range(parts):
         load_text(1, 0, k).wait()
@@ -204,10 +216,10 @@
     span = 2 * LANES
     step = 64
 
-    def meet(own, group, pair, k0, count, total, label, with_sums, fresh=False):
+    def meet(own, group, pieces, total, label, with_sums, joined=True, fresh=False, between=None):
         mine = held[own, 0, :, 0].reshape(rows, width)
-        for i in range(count):
-            other = held[group, pair, k0 + i].reshape(span, width)
+        for i, (pair, k) in enumerate(pieces):
+            other = held[group, pair, k].reshape(span, width)
             here = cosines.at[i % 2]
             here[...] = lax.dot_general(mine, other, NT, preferred_element_type=jnp.float32)
             for first in range(0, rows, step):
@@ -215,7 +227,7 @@
                 cosine = here[block]
                 logits = temp * cosine + shift
                 if label is not None:
-                    is_pair = label(first, k0 + i)
+                    is_pair = label(first, k)
                     logits = jnp.where(is_pair, -logits, logits)
                 small = jnp.exp(-jnp.abs(logits))
                 upper = 1.0 / (1.0 + small)
@@ -228,9 +240,17 @@
                     for j, value in enumerate((pair_loss, slope * cosine, slope)):
                         value = jnp.sum(value.reshape(step // 8, 8, span), axis=0)
                         sums[j * 8:(j + 1) * 8] += value[:, :LANES] + value[:, LANES:]
-        product = jnp.dot(slopes[:, :count * span], held[group, pair, pl.ds(k0, count)].reshape(count * span, width),
-                          preferred_element_type=jnp.float32)
-        total[...] = product if fresh else total[...] + product
+        if between is not None:
+            between()
+        if joined:
+            count = len(pieces)
+            (pair, k0) = pieces[0]
+            product = jnp.dot(slopes[:, :count * span], held[group, pair, pl.ds(k0, count)].reshape(count * span, width),
+                              preferred_element_type=jnp.float32)
+            total[...] = product if fresh else total[...] + product
+        else:
+            total[...] += sum(jnp.dot(slopes[:, i * span:(i + 1) * span], held[group, pair, k].reshape(span, width),
+                                      preferred_element_type=jnp.float32) for i, (pair, k) in enumerate(pieces))
 
     def text_meets_own(pair, k0, count, fresh=False):
         def label(first, k):
@@ -238,136 +258,152 @@
             at = jnp.concatenate([lane + quarter[pair][core] * rows for core in range(2)], axis=1)
             here = pos_cols[pl.ds(first, step)]
             return jnp.concatenate([here, here], axis=1) == at
-        meet(TXT, IMG, pair, k0, count, grad_text, label, True, fresh)
+        meet(TXT, IMG, [(pair, k0 + i) for i in range(count)], grad_text, label, True, fresh=fresh)
 
     def image_meets_own(pair, fresh=False):
         def label(first, k):
             at = lax.broadcasted_iota(jnp.int32, (step, span), 0) + (row * rows + first)
             return jnp.broadcast_to(pos_rows[pair, :, pl.ds(k * span, span)], (step, span)) == at
-        meet(IMG, TXT, pair, 0, parts, grad_image, label, False, fresh)
+        meet(IMG, TXT, [(pair, k) for k in range(parts)], grad_image, label, False, fresh=fresh)
 
     image_meets_own(0, True)
     text_meets_own(0, 0, parts, True)
     image_meets_own(1)
 
+    def bytes_of(ref, sent, arrived):
+        return pltpu.make_async_remote_copy(src_ref=ref, dst_ref=ref, send_sem=sent, recv_sem=arrived,
+                                            device_id=(dp, side), device_id_type=MESH)
+
     def to_a(i):
         return pltpu.make_async_remote_copy(
-            src_ref=sums, dst_ref=met_a.at[place_a], send_sem=send_a.at[i], recv_sem=recv_a.at[i],
+            src_ref=packed, dst_ref=met_a.at[place_a], send_sem=send_a, recv_sem=recv_a,
             device_id=group_a[i], device_id_type=MESH)
 
     def to_b(i):
         return pltpu.make_async_remote_copy(
-            src_ref=met_b.at[rest], dst_ref=met_b.at[rest], send_sem=send_b.at[i], recv_sem=recv_b.at[i],
+            src_ref=met_b.at[rest], dst_ref=met_b.at[rest], send_sem=send_b, recv_sem=recv_b,
             device_id=group_b[i], device_id_type=MESH)
 
-    @pl.loop(0, 2 * parts)
-    def _(s):
-        next_pair, next_k = jnp.where(last_z, s % 2, s // parts), jnp.where(last_z, s // 2, s % parts)
-        prev_pair, prev_k = jnp.where(first_z, s % 2, s // parts), jnp.where(first_z, s // 2, s % parts)
-        x_now = jnp.where(end_z, s % 2, 1 - s // parts) == 1
-        x_k = jnp.where(end_z, s // 2, s % parts)
-
-        @pl.when(x_now)
-        def _():
-            x_img(x_k).wait_recv()
-            f_img(x_k).start()
-
-            @pl.when(jnp.logical_not(end_z))
-            def _():
-                z_img(1, x_k).start()
-
-        z_img(next_pair, next_k).wait_recv()
-        f_next(next_pair, next_k).start()
-
-        @pl.when(jnp.logical_and(before_last_z, s < parts))
-        def _():
-            x_next(next_k).start()
-
-        z_txt(prev_pair, prev_k).wait_recv()
-        f_prev(prev_pair, prev_k).start()
-        f_next(next_pair, next_k).wait_recv()
-        meet(TXT, NEXT, next_pair, next_k, 1, grad_text, None, True)
-
-        @pl.when(x_now)
-        def _():
-            f_img(x_k).wait_recv()
-            text_meets_own(1, x_k, 1)
-
-        @pl.when(s == 2 * parts - 1)
-        def _():
-            for i in range(len(group_a)):
-                to_a(i).start()
-            met_a[place_a] = sums[...]
-
-        f_prev(prev_pair, prev_k).wait_recv()
-        meet(IMG, PREV, prev_pair, prev_k, 1, grad_image, None, False)
-
-    for i in range(len(group_a)):
-        to_a(i).wait_recv()
-    met_b[rest] = functools.reduce(lambda a, b: a + b, [met_a[i] for i in range(4 * n_y)])
-    for i in range(len(group_b)):
-        to_b(i).start()
-
-    own_text.wait()
-    own_image.wait()
-    for total, which in ((grad_text, 0), (grad_image, 1)):
+    def finish(total, which):
         @pl.loop(0, parts)
         def _(k):
             block = pl.ds(pl.multiple_of(k * LANES, LANES), LANES)
             full = raw[which, block].astype(jnp.float32)
             grad = temp * total[block]
-            inverse = lax.rsqrt(jnp.sum(full * full, axis=-1, keepdims=True) + 1e-06)
+            inverse = inverses[which, k][:, 0:1]
             unit = full * inverse
             along = jnp.sum(unit * grad, axis=-1, keepdims=True)
             total[block] = (grad - unit * along) * inverse
 
-    for i in range(len(group_b)):
-        to_b(i).wait_recv()
+    own_text.wait()
+    own_image.wait()
+    packed[...] = jnp.zeros_like(packed)
+
+    @pl.loop(0, parts)
+    def _(t):
+        def pieces(together):
+            return [(jnp.where(together, s % 2, s // parts), jnp.where(together, s // 2, s % parts))
+                    for s in (2 * t, 2 * t + 1)]
+
+        nexts, prevs = pieces(last_z), pieces(first_z)
+        early = t < parts // 2
+        x_two = jnp.logical_and(jnp.logical_not(end_z), early)
+
+        @pl.when(x_two)
+        def _():
+            for i in range(2):
+                x_img(2 * t + i).wait_recv()
+                f_img(2 * t + i).start()
+                z_img(1, 2 * t + i).start()
+
+        for i in range(2):
+            z_img(*nexts[i]).wait_recv()
+            f_next(*nexts[i]).start()
+
+            @pl.when(jnp.logical_and(before_last_z, early))
+            def _():
+                x_next(nexts[i][1]).start()
+
+            z_txt(*prevs[i]).wait_recv()
+            f_prev(*prevs[i]).start()
+
+        @pl.when(end_z)
+        def _():
+            x_img(t).wait_recv()
+            f_img(t).start()
+
+        @pl.when(x_two)
+        def _():
+            for i in range(2):
+                f_img(2 * t + i).wait_recv()
+            text_meets_own(1, 2 * t, 2)
+
+        @pl.when(end_z)
+        def _():
+            f_img(t).wait_recv()
+            text_meets_own(1, t, 1)
+
+        last = t == parts - 1
+
+        def start_sums():
+            @pl.when(last)
+            def _():
+                for i in range(3):
+                    packed[i:i + 1] = jnp.sum(sums[8 * i:8 * (i + 1)], axis=0, keepdims=True)
+                for i in range(len(group_a)):
+                    to_a(i).start()
+
+        for i in range(2):
+            f_next(*nexts[i]).wait_recv()
+        meet(TXT, NEXT, nexts, grad_text, None, True, joined=False, between=start_sums)
+
+        @pl.when(last)
+        def _():
+            finish(grad_text, 0)
+            met_a[place_a] = packed[...]
+            bytes_of(met_a.at[pl.ds(0, len(group_a))], send_a, recv_a).wait_recv()
+            met_b[rest] = functools.reduce(lambda a, b: a + b, [met_a[i] for i in range(4 * n_y)])
+            for i in range(len(group_b)):
+                to_b(i).start()
+
+        for i in range(2):
+            f_prev(*prevs[i]).wait_recv()
+        meet(IMG, PREV, prevs, grad_image, None, False, joined=False)
+
+    finish(grad_image, 1)
+    bytes_of(met_b.at[pl.ds(0, len(group_b))], send_b, recv_b).wait_recv()
     total = functools.reduce(lambda a, b: a + b, [met_b[i] for i in range(n_b)])
     count = rows * 4 * n_dp
-    out_sums[0] = jnp.sum(total[0:8]) / count
-    out_sums[1] = jnp.sum(temp * total[8:16]) / count
-    out_sums[2] = jnp.sum(total[16:24]) / count
-
-    @pl.loop(0, parts)
-    def _(k):
-        for made in (c_img, f_img):
-            made(k).wait_send()
-        for pair in range(2):
-            for made in (f_next, f_prev):
-                made(pair, k).wait_send()
-
-        @pl.when(sends_x)
-        def _():
-            x_img(k).wait_send()
-
-        @pl.when(x_for_side)
-        def _():
-            x_img_for_side(k).wait_send()
-
-        @pl.when(before_last_z)
-        def _():
-            x_next(k).wait_send()
-
-        for sends, for_side, made, made_for_side in (
-                (sends_img, img_for_side, z_img, z_img_for_side), (sends_txt, txt_for_side, z_txt, z_txt_for_side)):
-            @pl.when(sends)
-            def _():
-                made(0, k).wait_send()
-
-            @pl.when(jnp.logical_and(sends, jnp.logical_not(last_z)) if made is z_img else sends)
-            def _():
-                made(1, k).wait_send()
-
-            @pl.when(for_side)
-            def _():
-                for pair in range(2):
-                    made_for_side(pair, k).wait_send()
-
-    for i in range(len(group_a)):
-        to_a(i).wait_send()
-    for i in range(len(group_b)):
-        to_b(i).wait_send()
+    out_sums[...] = total / count
+    out_sums[1:2] = temp * total[1:2] / count
+
+    def all_sent(*kinds):
+        for kind in kinds:
+            bytes_of(raw.at[0], send_sem.at[kind], recv_sem.at[0, 0]).wait_send()
+
+    all_sent(C_IMG, F_IMG, F_NEXT, F_NEXT + 1, F_PREV, F_PREV + 1)
+    for sends, kinds in ((sends_x, (X_IMG,)), (x_for_side, (FOR_SIDE,)), (before_last_z, (X_NEXT,)),
+                         (sends_img, (Z_IMG,)), (jnp.logical_and(sends_img, jnp.logical_not(last_z)), (Z_IMG + 1,)),
+                         (img_for_side, (FOR_SIDE + 1, FOR_SIDE + 2)),
+                         (sends_txt, (Z_TXT, Z_TXT + 1)), (txt_for_side, (FOR_SIDE + 1, FOR_SIDE + 2))):
+        @pl.when(sends)
+        def _():
+            all_sent(*kinds)
+
+    bytes_of(met_a.at[pl.ds(0, len(group_a))], send_a, recv_a).wait_send()
+    bytes_of(met_b.at[pl.ds(0, len(group_b))], send_b, recv_b).wait_send()
+
+
+def write_out(grad_text, grad_image, sums, out_text, out_image, loss, grad_log_temp, grad_bias, sem):
+    half = grad_text.shape[0] // 2
+    copies = [pltpu.make_async_copy(source.at[pl.ds(i * half, half)], target.at[pl.ds(i * half, half)], sem.at[2 * j + i])
+              for j, (source, target) in enumerate(((grad_text, out_text), (grad_image, out_image))) for i in range(2)]
+    for copy in copies:
+        copy.start()
+    for j, out in enumerate((loss, grad_log_temp, grad_bias)):
+        out[0] = jnp.sum(sums[j:j + 1])
+    for copy in copies:
+        copy.wait()
 
 
 def on_device(n_dp, text, image, positive, log_temp, bias):
@@ -377,28 +413,30 @@
     n_a = 4 * (n_dp // n_b)
     vmem, smem, hbm = (pl.BlockSpec(memory_space=m) for m in (pltpu.VMEM, pltpu.SMEM, pltpu.HBM))
     dma = pltpu.SemaphoreType.DMA
-    grad_text, grad_image, totals = pl.pallas_call(
+    results = pl.pallas_call(
         functools.partial(kernel, n_dp),
         out_shape=(
             jax.ShapeDtypeStruct((rows, width), jnp.float32),
             jax.ShapeDtypeStruct((rows, width), jnp.float32),
-            jax.ShapeDtypeStruct((3,), jnp.float32),
+            jax.ShapeDtypeStruct((8, LANES), jnp.float32),
         ),
         in_specs=[hbm, hbm, hbm, smem, smem],
-        out_specs=(vmem, vmem, smem),
+        out_specs=(vmem, vmem, vmem),
         scratch_shapes=[
             pltpu.VMEM((4, 2, parts, 2, LANES, width), jnp.bfloat16),
             pltpu.VMEM((2, rows, width), jnp.bfloat16),
+            pltpu.VMEM((2, parts, LANES, LANES), jnp.float32),
             pltpu.VMEM((2, rows, 2 * LANES), jnp.float32),
             pltpu.VMEM((rows, 2 * rows), jnp.bfloat16),
             pltpu.VMEM((1, 4 * rows), jnp.int32),
             pltpu.VMEM((rows, LANES), jnp.int32),
             pltpu.VMEM((2, 1, 2 * rows), jnp.int32),
             pltpu.VMEM((24, LANES), jnp.float32),
-            pltpu.VMEM((n_a, 24, LANES), jnp.float32),
-            pltpu.VMEM((n_b, 24, LANES), jnp.float32),
-            dma((5, parts)), dma((3,)), dma((KINDS + 4, parts)), dma((KINDS, parts)),
-            dma((n_a,)), dma((n_a,)), dma((n_b,)), dma((n_b,)),
+            pltpu.VMEM((8, LANES), jnp.float32),
+            pltpu.VMEM((n_a, 8, LANES), jnp.float32),
+            pltpu.VMEM((n_b, 8, LANES), jnp.float32),
+            dma((5, parts)), dma((3,)), dma((KINDS + 4,)), dma((KINDS, parts)),
+            *(dma(()),) * 4,
         ],
         compiler_params=pltpu.CompilerParams(
             collective_id=0, has_side_effects=True, vmem_limit_bytes=48 * 1024 * 1024),
@@ -406,7 +444,15 @@
             flops=2 * 32 * rows * rows * width, bytes_accessed=7 * rows * width * 2 + 2 * rows * width * 4,
             transcendentals=24 * rows * rows),
     )(text, image, positive, log_temp, bias)
-    return grad_text, grad_image, totals[0:1], totals[1:2], totals[2:3]
+    scalar = jax.ShapeDtypeStruct((1,), jnp.float32)
+    return pl.pallas_call(
+        write_out,
+        out_shape=(*(jax.ShapeDtypeStruct((rows, width), jnp.float32),) * 2, scalar, scalar, scalar),
+        in_specs=[vmem, vmem, vmem],
+        out_specs=(hbm, hbm, smem, smem, smem),
+        scratch_shapes=[dma((4,))],
+        compiler_params=pltpu.CompilerParams(vmem_limit_bytes=1024 * 1024),
+    )(*results)
 
 
 def solution(mesh):

time: 93.2 us -> 85.9 us (0.922)
  Pallas kernels: 85.7 us -> 81.7 us
  local copies, waits for them, and re-layouts: 5.36 us -> 1.96 us
    pallas_call x1, Pallas kernels: 85.7 us -> 78.9 us  [on_device(): pl.pallas_call(functools.partial(kernel, n_dp), out_shape=(jax.ShapeDtype...]
    unnamed x6 -> x4, local copies, waits for them, and re-layouts: 4.77 us -> 1.96 us
    pallas_call x0 -> x1, Pallas kernels: none -> 2.75 us  [on_device(): pl.pallas_call(write_out, out_shape=(*(jax.ShapeDtypeStruct((rows, width)...]
where the time goes in v3:
time: 85.9 us; the launch traced here: 85.7 us
  Pallas kernels  81.7 us (95%)
  between operations  2.1 us (2%)
  local copies, waits for them, and re-layouts  1.96 us (2%)
    pallas_call x1, Pallas kernels, on_device(): pl.pallas_call(functools.partial(kernel, n_dp), out_shape=(jax.ShapeDtype...  78.9 us
    pallas_call x1, Pallas kernels, on_device(): pl.pallas_call(write_out, out_shape=(*(jax.ShapeDtypeStruct((rows, width)...  2.75 us
    unnamed x4, local copies, waits for them, and re-layouts  1.96 us

profile of v3, /device:TPU:1, one launch (start us, length us, event | category | flops | bytes accessed | tf_op | source)
XLA Modules:
  0.0 85.7 jit_solution(13541804635454489757)
XLA Ops:
  1.9 0.0 copy-start
  1.9 1.3 %copy-done = bf16[512,1152]{1,0:T(8,128)(2,1)S(1)} copy-done((bf16[512,1152]{1,0:T(8,128)(2,1)S(1)}, bf16[512,1152]{1,0:T(8,128)(2,1)}, u32[]{:S(2)}) %copy-start) | copy-done | bytes 1179672
  3.2 0.0 copy-start.1
  3.2 0.7 copy-done.1
  3.9 78.9 %shard_map.92 = (f32[512,1152]{1,0:T(8,128)S(1)}, f32[512,1152]{1,0:T(8,128)S(1)}, f32[8,128]{1,0:T(8,128)S(1)}) custom-call(bf16[2048,1152]{1,0:T(8,128)(2,1)} %text.1, bf16[512,1152]{1,0:T(8,128)(2,1)S(1)} %copy-done, s32[1,2048]{1,0:T(1,128)S(1)} %copy-done.1, f32[1]{0:T(128)S(6)} %copy.10.log_temp, f32[1]{0:T(128)S(6)} %copy.11.bias), custom_call_target="tpu_custom_call" | custom-call | flops 19327352832 | bytes 12976128 | tf_op jit(solution)/shard_map/pallas_call | solution.py:416
  82.8 2.8 %shard_map.93 = (f32[512,1152]{1,0:T(8,128)}, f32[512,1152]{1,0:T(8,128)}, f32[1]{0:T(128)}, f32[1]{0:T(128)}, f32[1]{0:T(128)}) custom-call(f32[512,1152]{1,0:T(8,128)S(1)} %get-tuple-element.8.grad_text, f32[512,1152]{1,0:T(8,128)S(1)} %get-tuple-element.9.grad_image, f32[8,128]{1,0:T(8,128)S(1)} %get-tuple-element.10.sums), custom_call_target="tpu_custom_call" | custom-call | tf_op jit(solution)/shard_map/pallas_call | solution.py:448
Async XLA Ops:
  1.9 1.3 %copy-start = (bf16[512,1152]{1,0:T(8,128)(2,1)S(1)}, bf16[512,1152]{1,0:T(8,128)(2,1)}, u32[]{:S(2)}) copy-start(bf16[512,1152]{1,0:T(8,128)(2,1)} %image.1) | copy-start | bytes 3538948
  3.2 0.7 copy-start.1

commit v4 on v3

--- a/solution.py
+++ b/solution.py
@@ -216,12 +216,15 @@
     span = 2 * LANES
     step = 64
 
-    def meet(own, group, pieces, total, label, with_sums, joined=True, fresh=False, between=None):
+    def meet(own, group, pieces, total, label, with_sums, fresh=False, between=None):
         mine = held[own, 0, :, 0].reshape(rows, width)
+        others = jnp.concatenate([held[group, pair, k].reshape(span, width) for pair, k in pieces], axis=0)
+        if len(pieces) <= 2:
+            cosines[:, :len(pieces) * span] = lax.dot_general(mine, others, NT, preferred_element_type=jnp.float32)
         for i, (pair, k) in enumerate(pieces):
-            other = held[group, pair, k].reshape(span, width)
-            here = cosines.at[i % 2]
-            here[...] = lax.dot_general(mine, other, NT, preferred_element_type=jnp.float32)
+            here = cosines.at[:, pl.ds((i % 2) * span, span)]
+            if len(pieces) > 2 and i % 2 == 0:
+                cosines[...] = lax.dot_general(mine, others[i * span:(i + 2) * span], NT, preferred_element_type=jnp.float32)
             for first in range(0, rows, step):
                 block = pl.ds(first, step)
                 cosine = here[block]
@@ -242,15 +245,8 @@
                         sums[j * 8:(j + 1) * 8] += value[:, :LANES] + value[:, LANES:]
         if between is not None:
             between()
-        if joined:
-            count = len(pieces)
-            (pair, k0) = pieces[0]
-            product = jnp.dot(slopes[:, :count * span], held[group, pair, pl.ds(k0, count)].reshape(count * span, width),
-                              preferred_element_type=jnp.float32)
-            total[...] = product if fresh else total[...] + product
-        else:
-            total[...] += sum(jnp.dot(slopes[:, i * span:(i + 1) * span], held[group, pair, k].reshape(span, width),
-                                      preferred_element_type=jnp.float32) for i, (pair, k) in enumerate(pieces))
+        product = jnp.dot(slopes[:, :len(pieces) * span], others, preferred_element_type=jnp.float32)
+        total[...] = product if fresh else total[...] + product
 
     def text_meets_own(pair, k0, count, fresh=False):
         def label(first, k):
@@ -316,21 +312,34 @@
                 f_img(2 * t + i).start()
                 z_img(1, 2 * t + i).start()
 
-        for i in range(2):
-            z_img(*nexts[i]).wait_recv()
-            f_next(*nexts[i]).start()
-
-            @pl.when(jnp.logical_and(before_last_z, early))
-            def _():
-                x_next(nexts[i][1]).start()
-
-            z_txt(*prevs[i]).wait_recv()
-            f_prev(*prevs[i]).start()
+        def take_nexts():
+            for i in range(2):
+                z_img(*nexts[i]).wait_recv()
+                f_next(*nexts[i]).start()
+
+                @pl.when(jnp.logical_and(before_last_z, early))
+                def _():
+                    x_next(nexts[i][1]).start()
+
+        def take_prevs():
+            for i in range(2):
+                z_txt(*prevs[i]).wait_recv()
+                f_prev(*prevs[i]).start()
+
+        def meet_prevs():
+            for i in range(2):
+                f_prev(*prevs[i]).wait_recv()
+            meet(IMG, PREV, prevs, grad_image, None, False)
+
+        pl.when(jnp.logical_not(last_z))(take_nexts)
+        pl.when(jnp.logical_not(first_z))(take_prevs)
 
         @pl.when(end_z)
         def _():
             x_img(t).wait_recv()
             f_img(t).start()
+
+        pl.when(last_z)(meet_prevs)
 
         @pl.when(x_two)
         def _():
@@ -353,9 +362,11 @@
                 for i in range(len(group_a)):
                     to_a(i).start()
 
+        pl.when(last_z)(take_nexts)
         for i in range(2):
             f_next(*nexts[i]).wait_recv()
-        meet(TXT, NEXT, nexts, grad_text, None, True, joined=False, between=start_sums)
+        meet(TXT, NEXT, nexts, grad_text, None, True, between=start_sums)
+        pl.when(first_z)(take_prevs)
 
         @pl.when(last)
         def _():
@@ -366,9 +377,7 @@
             for i in range(len(group_b)):
                 to_b(i).start()
 
-        for i in range(2):
-            f_prev(*prevs[i]).wait_recv()
-        meet(IMG, PREV, prevs, grad_image, None, False, joined=False)
+        pl.when(jnp.logical_not(last_z))(meet_prevs)
 
     finish(grad_image, 1)
     bytes_of(met_b.at[pl.ds(0, len(group_b))], send_b, recv_b).wait_recv()
@@ -426,7 +435,7 @@
             pltpu.VMEM((4, 2, parts, 2, LANES, width), jnp.bfloat16),
             pltpu.VMEM((2, rows, width), jnp.bfloat16),
             pltpu.VMEM((2, parts, LANES, LANES), jnp.float32),
-            pltpu.VMEM((2, rows, 2 * LANES), jnp.float32),
+            pltpu.VMEM((rows, 4 * LANES), jnp.float32),
             pltpu.VMEM((rows, 2 * rows), jnp.bfloat16),
             pltpu.VMEM((1, 4 * rows), jnp.int32),
             pltpu.VMEM((rows, LANES), jnp.int32),

time: 85.9 us -> 84.7 us (0.986)
  Pallas kernels: 81.7 us -> 80.4 us
    pallas_call x1, Pallas kernels: 78.9 us -> 77.7 us  [on_device(): pl.pallas_call(functools.partial(kernel, n_dp), out_shape=(jax.ShapeDtype...]
where the time goes in v4:
time: 84.7 us; the launch traced here: 84.5 us
  Pallas kernels  80.4 us (95%)
  between operations  2.1 us (2%)
  local copies, waits for them, and re-layouts  1.96 us (2%)
    pallas_call x1, Pallas kernels, on_device(): pl.pallas_call(functools.partial(kernel, n_dp), out_shape=(jax.ShapeDtype...  77.7 us
    pallas_call x1, Pallas kernels, on_device(): pl.pallas_call(write_out, out_shape=(*(jax.ShapeDtypeStruct((rows, width)...  2.75 us
    unnamed x4, local copies, waits for them, and re-layouts  1.96 us

profile of v4, /device:TPU:1, one launch (start us, length us, event | category | flops | bytes accessed | tf_op | source)
XLA Modules:
  0.0 84.5 jit_solution(6674494704753188693)
XLA Ops:
  1.9 0.0 copy-start
  1.9 1.3 %copy-done = bf16[512,1152]{1,0:T(8,128)(2,1)S(1)} copy-done((bf16[512,1152]{1,0:T(8,128)(2,1)S(1)}, bf16[512,1152]{1,0:T(8,128)(2,1)}, u32[]{:S(2)}) %copy-start) | copy-done | bytes 1179672
  3.2 0.0 copy-start.1
  3.2 0.7 copy-done.1
  3.9 77.7 %shard_map.92 = (f32[512,1152]{1,0:T(8,128)S(1)}, f32[512,1152]{1,0:T(8,128)S(1)}, f32[8,128]{1,0:T(8,128)S(1)}) custom-call(bf16[2048,1152]{1,0:T(8,128)(2,1)} %text.1, bf16[512,1152]{1,0:T(8,128)(2,1)S(1)} %copy-done, s32[1,2048]{1,0:T(1,128)S(1)} %copy-done.1, f32[1]{0:T(128)S(6)} %copy.10.log_temp, f32[1]{0:T(128)S(6)} %copy.11.bias), custom_call_target="tpu_custom_call" | custom-call | flops 19327352832 | bytes 12976128 | tf_op jit(solution)/shard_map/pallas_call | solution.py:425
  81.6 2.8 %shard_map.93 = (f32[512,1152]{1,0:T(8,128)}, f32[512,1152]{1,0:T(8,128)}, f32[1]{0:T(128)}, f32[1]{0:T(128)}, f32[1]{0:T(128)}) custom-call(f32[512,1152]{1,0:T(8,128)S(1)} %get-tuple-element.8.grad_text, f32[512,1152]{1,0:T(8,128)S(1)} %get-tuple-element.9.grad_image, f32[8,128]{1,0:T(8,128)S(1)} %get-tuple-element.10.sums), custom_call_target="tpu_custom_call" | custom-call | tf_op jit(solution)/shard_map/pallas_call | solution.py:457
Async XLA Ops:
  1.9 1.3 %copy-start = (bf16[512,1152]{1,0:T(8,128)(2,1)S(1)}, bf16[512,1152]{1,0:T(8,128)(2,1)}, u32[]{:S(2)}) copy-start(bf16[512,1152]{1,0:T(8,128)(2,1)} %image.1) | copy-start | bytes 3538948
  3.2 0.7 copy-start.1

commit v5 on v4

--- a/solution.py
+++ b/solution.py
@@ -50,32 +50,26 @@
     def load(source, first, group, pair, k, core):
         first = pl.multiple_of(first + k * LANES, LANES)
         return pltpu.make_async_copy(source.at[pl.ds(first, LANES)], held.at[group, pair, k, core],
-                                     load_sem.at[0 if group == IMG else 1 + 2 * pair + core, k])
-
-    def load_image(k):
-        return load(image, 0, IMG, 0, k, 0)
+                                     load_sem.at[2 * pair + core, k])
 
     def load_text(pair, core, k):
         return load(text, quarter[pair][core] * rows, TXT, pair, k, core)
 
-    for k in range(parts):
-        load_image(k).start()
-    pos_copy = pltpu.make_async_copy(positive, pos, raw_sem.at[2])
+    pos_copy = pltpu.make_async_copy(positive, pos, raw_sem.at[1])
     for pair, core in ((0, 0), (1, 0), (0, 1), (1, 1)):
         for k in range(parts):
             load_text(pair, core, k).start()
         if core == 0 and pair == 1:
             pos_copy.start()
-    own_text = pltpu.make_async_copy(text.at[pl.ds(pl.multiple_of(row * rows, rows), rows)], raw.at[0], raw_sem.at[0])
-    own_image = pltpu.make_async_copy(image, raw.at[1], raw_sem.at[1])
+    own_text = pltpu.make_async_copy(text.at[pl.ds(pl.multiple_of(row * rows, rows), rows)], raw, raw_sem.at[0])
     own_text.start()
-    own_image.start()
 
     temp = jnp.exp(jnp.full((8, LANES), log_temp[0], jnp.float32))[0:1, 0:1]
     shift = bias[0]
 
     def normalise(group, pair, k, core):
-        full = held[group, pair, k, core].astype(jnp.float32)
+        source = image[k * LANES:(k + 1) * LANES] if group == IMG else held[group, pair, k, core]
+        full = source.astype(jnp.float32)
         inverse = lax.rsqrt(jnp.sum(full * full, axis=-1, keepdims=True) + 1e-06)
         held[group, pair, k, core] = (full * inverse).astype(jnp.bfloat16)
         if pair == 0 and core == 0:
@@ -134,7 +128,6 @@
     x_for_side = jnp.logical_and(end_z, core1)
 
     for k in range(parts):
-        load_image(k).wait()
         normalise(IMG, 0, k, 0)
         if k == 0:
             pl.semaphore_wait(barrier, len(greeted))
@@ -284,7 +277,7 @@
         @pl.loop(0, parts)
         def _(k):
             block = pl.ds(pl.multiple_of(k * LANES, LANES), LANES)
-            full = raw[which, block].astype(jnp.float32)
+            full = (raw, image)[which][block].astype(jnp.float32)
             grad = temp * total[block]
             inverse = inverses[which, k][:, 0:1]
             unit = full * inverse
@@ -292,7 +285,6 @@
             total[block] = (grad - unit * along) * inverse
 
     own_text.wait()
-    own_image.wait()
     packed[...] = jnp.zeros_like(packed)
 
     @pl.loop(0, parts)
@@ -330,27 +322,6 @@
             for i in range(2):
                 f_prev(*prevs[i]).wait_recv()
             meet(IMG, PREV, prevs, grad_image, None, False)
-
-        pl.when(jnp.logical_not(last_z))(take_nexts)
-        pl.when(jnp.logical_not(first_z))(take_prevs)
-
-        @pl.when(end_z)
-        def _():
-            x_img(t).wait_recv()
-            f_img(t).start()
-
-        pl.when(last_z)(meet_prevs)
-
-        @pl.when(x_two)
-        def _():
-            for i in range(2):
-                f_img(2 * t + i).wait_recv()
-            text_meets_own(1, 2 * t, 2)
-
-        @pl.when(end_z)
-        def _():
-            f_img(t).wait_recv()
-            text_meets_own(1, t, 1)
 
         last = t == parts - 1
 
@@ -362,11 +333,37 @@
                 for i in range(len(group_a)):
                     to_a(i).start()
 
+        def meet_nexts(between=None):
+            for i in range(2):
+                f_next(*nexts[i]).wait_recv()
+            meet(TXT, NEXT, nexts, grad_text, None, True, between=between)
+
+        pl.when(jnp.logical_not(last_z))(take_nexts)
+        pl.when(jnp.logical_not(first_z))(take_prevs)
+        pl.when(last_z)(meet_prevs)
+        pl.when(jnp.logical_not(last_z))(meet_nexts)
+
+        @pl.when(x_two)
+        def _():
+            for i in range(2):
+                f_img(2 * t + i).wait_recv()
+            text_meets_own(1, 2 * t, 2)
+
+        @pl.when(end_z)
+        def _():
+            x_img(t).wait_recv()
+            f_img(t).start()
+
+        pl.when(first_z)(take_prevs)
         pl.when(last_z)(take_nexts)
-        for i in range(2):
-            f_next(*nexts[i]).wait_recv()
-        meet(TXT, NEXT, nexts, grad_text, None, True, between=start_sums)
-        pl.when(first_z)(take_prevs)
+
+        @pl.when(end_z)
+        def _():
+            f_img(t).wait_recv()
+            text_meets_own(1, t, 1)
+
+        pl.when(last_z)(functools.partial(meet_nexts, start_sums))
+        pl.when(jnp.logical_not(last_z))(start_sums)
 
         @pl.when(last)
         def _():
@@ -388,7 +385,7 @@
 
     def all_sent(*kinds):
         for kind in kinds:
-            bytes_of(raw.at[0], send_sem.at[kind], recv_sem.at[0, 0]).wait_send()
+            bytes_of(raw, send_sem.at[kind], recv_sem.at[0, 0]).wait_send()
 
     all_sent(C_IMG, F_IMG, F_NEXT, F_NEXT + 1, F_PREV, F_PREV + 1)
     for sends, kinds in ((sends_x, (X_IMG,)), (x_for_side, (FOR_SIDE,)), (before_last_z, (X_NEXT,)),
@@ -404,9 +401,9 @@
 
 
 def write_out(grad_text, grad_image, sums, out_text, out_image, loss, grad_log_temp, grad_bias, sem):
-    half = grad_text.shape[0] // 2
-    copies = [pltpu.make_async_copy(source.at[pl.ds(i * half, half)], target.at[pl.ds(i * half, half)], sem.at[2 * j + i])
-              for j, (source, target) in enumerate(((grad_text, out_text), (grad_image, out_image))) for i in range(2)]
+    part = grad_text.shape[0] // 4
+    copies = [pltpu.make_async_copy(source.at[pl.ds(i * part, part)], target.at[pl.ds(i * part, part)], sem.at[4 * j + i])
+              for j, (source, target) in enumerate(((grad_text, out_text), (grad_image, out_image))) for i in range(4)]
     for copy in copies:
         copy.start()
     for j, out in enumerate((loss, grad_log_temp, grad_bias)):
@@ -429,11 +426,11 @@
             jax.ShapeDtypeStruct((rows, width), jnp.float32),
             jax.ShapeDtypeStruct((8, LANES), jnp.float32),
         ),
-        in_specs=[hbm, hbm, hbm, smem, smem],
+        in_specs=[hbm, vmem, hbm, smem, smem],
         out_specs=(vmem, vmem, vmem),
         scratch_shapes=[
             pltpu.VMEM((4, 2, parts, 2, LANES, width), jnp.bfloat16),
-            pltpu.VMEM((2, rows, width), jnp.bfloat16),
+            pltpu.VMEM((rows, width), jnp.bfloat16),
             pltpu.VMEM((2, parts, LANES, LANES), jnp.float32),
             pltpu.VMEM((rows, 4 * LANES), jnp.float32),
             pltpu.VMEM((rows, 2 * rows), jnp.bfloat16),
@@ -444,7 +441,7 @@
             pltpu.VMEM((8, LANES), jnp.float32),
             pltpu.VMEM((n_a, 8, LANES), jnp.float32),
             pltpu.VMEM((n_b, 8, LANES), jnp.float32),
-            dma((5, parts)), dma((3,)), dma((KINDS + 4,)), dma((KINDS, parts)),
+            dma((4, parts)), dma((2,)), dma((KINDS + 4,)), dma((KINDS, parts)),
             *(dma(()),) * 4,
         ],
         compiler_params=pltpu.CompilerParams(
@@ -459,7 +456,7 @@
         out_shape=(*(jax.ShapeDtypeStruct((rows, width), jnp.float32),) * 2, scalar, scalar, scalar),
         in_specs=[vmem, vmem, vmem],
         out_specs=(hbm, hbm, smem, smem, smem),
-        scratch_shapes=[dma((4,))],
+        scratch_shapes=[dma((8,))],
         compiler_params=pltpu.CompilerParams(vmem_limit_bytes=1024 * 1024),
     )(*results)
 

time: 84.7 us -> 84.3 us (level)
  no operation moved by 1% of the time
where the time goes in v5:
time: 84.3 us; the launch traced here: 84.1 us
  Pallas kernels  80 us (95%)
  between operations  2.1 us (2%)
  local copies, waits for them, and re-layouts  1.96 us (2%)
    pallas_call x1, Pallas kernels, on_device(): pl.pallas_call(functools.partial(kernel, n_dp), out_shape=(jax.ShapeDtype...  77.3 us
    pallas_call x1, Pallas kernels, on_device(): pl.pallas_call(write_out, out_shape=(*(jax.ShapeDtypeStruct((rows, width)...  2.78 us
    unnamed x4, local copies, waits for them, and re-layouts  1.96 us

profile of v5, /device:TPU:1, one launch (start us, length us, event | category | flops | bytes accessed | tf_op | source)
XLA Modules:
  0.0 84.1 jit_solution(9704026741053412737)
XLA Ops:
  1.9 0.0 copy-start
  1.9 1.3 %copy-done = bf16[512,1152]{1,0:T(8,128)(2,1)S(1)} copy-done((bf16[512,1152]{1,0:T(8,128)(2,1)S(1)}, bf16[512,1152]{1,0:T(8,128)(2,1)}, u32[]{:S(2)}) %copy-start) | copy-done | bytes 1179672
  3.2 0.0 copy-start.1
  3.2 0.7 copy-done.1
  3.9 77.3 %shard_map.92 = (f32[512,1152]{1,0:T(8,128)S(1)}, f32[512,1152]{1,0:T(8,128)S(1)}, f32[8,128]{1,0:T(8,128)S(1)}) custom-call(bf16[2048,1152]{1,0:T(8,128)(2,1)} %text.1, bf16[512,1152]{1,0:T(8,128)(2,1)S(1)} %copy-done, s32[1,2048]{1,0:T(1,128)S(1)} %copy-done.1, f32[1]{0:T(128)S(6)} %copy.10.log_temp, f32[1]{0:T(128)S(6)} %copy.11.bias), custom_call_target="tpu_custom_call" | custom-call | flops 19327352832 | bytes 12976128 | tf_op jit(solution)/shard_map/pallas_call | solution.py:422
  81.2 2.8 %shard_map.93 = (f32[512,1152]{1,0:T(8,128)}, f32[512,1152]{1,0:T(8,128)}, f32[1]{0:T(128)}, f32[1]{0:T(128)}, f32[1]{0:T(128)}) custom-call(f32[512,1152]{1,0:T(8,128)S(1)} %get-tuple-element.8.grad_text, f32[512,1152]{1,0:T(8,128)S(1)} %get-tuple-element.9.grad_image, f32[8,128]{1,0:T(8,128)S(1)} %get-tuple-element.10.sums), custom_call_target="tpu_custom_call" | custom-call | tf_op jit(solution)/shard_map/pallas_call | solution.py:454
Async XLA Ops:
  1.9 1.3 %copy-start = (bf16[512,1152]{1,0:T(8,128)(2,1)S(1)}, bf16[512,1152]{1,0:T(8,128)(2,1)}, u32[]{:S(2)}) copy-start(bf16[512,1152]{1,0:T(8,128)(2,1)} %image.1) | copy-start | bytes 3538948
  3.2 0.7 copy-start.1

commit v6 on v5

--- a/solution.py
+++ b/solution.py
@@ -127,10 +127,28 @@
     txt_for_side = jnp.logical_and(last_z, core0)
     x_for_side = jnp.logical_and(end_z, core1)
 
+    def send_texts(k):
+        load_text(0, 0, k).wait()
+        normalise(TXT, 0, k, 0)
+
+        @pl.when(sends_txt)
+        def _():
+            z_txt(0, k).start()
+
+        load_text(0, 1, k).wait()
+        normalise(TXT, 0, k, 1)
+
+        @pl.when(txt_for_side)
+        def _():
+            z_txt(1, k).start()
+            z_txt_for_side(0, k).start()
+            z_txt_for_side(1, k).start()
+
     for k in range(parts):
         normalise(IMG, 0, k, 0)
         if k == 0:
             pl.semaphore_wait(barrier, len(greeted))
+            pl.when(last_z)(functools.partial(send_texts, 0))
         c_img(k).start()
 
         @pl.when(jnp.logical_not(end_z))
@@ -152,21 +170,10 @@
                 x_img(k).start()
 
     for k in range(parts):
-        load_text(0, 0, k).wait()
-        normalise(TXT, 0, k, 0)
-
-        @pl.when(sends_txt)
-        def _():
-            z_txt(0, k).start()
-
-        load_text(0, 1, k).wait()
-        normalise(TXT, 0, k, 1)
-
-        @pl.when(txt_for_side)
-        def _():
-            z_txt(1, k).start()
-            z_txt_for_side(0, k).start()
-            z_txt_for_side(1, k).start()
+        if k == 0:
+            pl.when(jnp.logical_not(last_z))(functools.partial(send_texts, 0))
+        else:
+            send_texts(k)
 
         c_img(k).wait_recv()
 

time: 84.3 us -> 84.3 us (level)
  no operation moved by 1% of the time
where the time goes in v6:
time: 84.3 us; the launch traced here: 84.1 us
  Pallas kernels  80 us (95%)
  between operations  2.1 us (2%)
  local copies, waits for them, and re-layouts  1.96 us (2%)
    pallas_call x1, Pallas kernels, on_device(): pl.pallas_call(functools.partial(kernel, n_dp), out_shape=(jax.ShapeDtype...  77.3 us
    pallas_call x1, Pallas kernels, on_device(): pl.pallas_call(write_out, out_shape=(*(jax.ShapeDtypeStruct((rows, width)...  2.78 us
    unnamed x4, local copies, waits for them, and re-layouts  1.96 us

profile of v6, /device:TPU:1, one launch (start us, length us, event | category | flops | bytes accessed | tf_op | source)
XLA Modules:
  0.0 84.1 jit_solution(17308877414173324867)
XLA Ops:
  1.9 0.0 copy-start
  1.9 1.3 %copy-done = bf16[512,1152]{1,0:T(8,128)(2,1)S(1)} copy-done((bf16[512,1152]{1,0:T(8,128)(2,1)S(1)}, bf16[512,1152]{1,0:T(8,128)(2,1)}, u32[]{:S(2)}) %copy-start) | copy-done | bytes 1179672
  3.2 0.0 copy-start.1
  3.2 0.7 copy-done.1
  3.9 77.3 %shard_map.92 = (f32[512,1152]{1,0:T(8,128)S(1)}, f32[512,1152]{1,0:T(8,128)S(1)}, f32[8,128]{1,0:T(8,128)S(1)}) custom-call(bf16[2048,1152]{1,0:T(8,128)(2,1)} %text.1, bf16[512,1152]{1,0:T(8,128)(2,1)S(1)} %copy-done, s32[1,2048]{1,0:T(1,128)S(1)} %copy-done.1, f32[1]{0:T(128)S(6)} %copy.10.log_temp, f32[1]{0:T(128)S(6)} %copy.11.bias), custom_call_target="tpu_custom_call" | custom-call | flops 19327352832 | bytes 12976128 | tf_op jit(solution)/shard_map/pallas_call | solution.py:429
  81.2 2.8 %shard_map.93 = (f32[512,1152]{1,0:T(8,128)}, f32[512,1152]{1,0:T(8,128)}, f32[1]{0:T(128)}, f32[1]{0:T(128)}, f32[1]{0:T(128)}) custom-call(f32[512,1152]{1,0:T(8,128)S(1)} %get-tuple-element.8.grad_text, f32[512,1152]{1,0:T(8,128)S(1)} %get-tuple-element.9.grad_image, f32[8,128]{1,0:T(8,128)S(1)} %get-tuple-element.10.sums), custom_call_target="tpu_custom_call" | custom-call | tf_op jit(solution)/shard_map/pallas_call | solution.py:461
Async XLA Ops:
  1.9 1.3 %copy-start = (bf16[512,1152]{1,0:T(8,128)(2,1)S(1)}, bf16[512,1152]{1,0:T(8,128)(2,1)}, u32[]{:S(2)}) copy-start(bf16[512,1152]{1,0:T(8,128)(2,1)} %image.1) | copy-start | bytes 3538948
  3.2 0.7 copy-start.1
